TPU v7x, 256 devices: a whole 4x4x8 slice. The times are simulated.
256 devices in a mesh: rows: 32 (over z, y), cols: 8 (over x, core).
Axes of the slice: x: 4, y: 4, z: 8, core: 2. Of those that a mesh axis runs over, the one named last changes fastest.
Arguments:
- genotypes: float32 [294912, 2048], P('rows', 'cols'), as said below
- right_sides: float32 [294912, 64], P(('rows', 'cols')), may hold values from -6 to 6
- inverse_r: float32 [2048, 2048], P('cols'), as said below
Outputs:
- solution: float32 [2048, 64], P('cols')
- last_basis: float32 [294912, 64], P(('rows', 'cols'))
Inputs may be any that keep to these rules, and one draw needn't show every extreme that they name: `genotypes`: each column is a genotype count of 0, 1 or 2, centred by its allele frequency and scaled per column. `inverse_r`: upper triangular with a diagonal between 1 and 2.
All inputs are finite; a program needn't handle non-finite values.
Results may differ from a plain program's by a relative error of at most 0.0003.
Values sent between devices are 32-bit elements; how exact they have to be, the bound alone decides.
A program may use at most 64 MiB of HBM per device.

v0:
```python
import jax
import jax.numpy as jnp
from jax import lax
from jax.sharding import PartitionSpec as P

ITERS = 2


def product(left, right):
    return jnp.dot(left, right, precision=lax.Precision.HIGHEST, preferred_element_type=jnp.float32)


def orthonormal(lower_factor, block):
    return jax.scipy.linalg.solve_triangular(lower_factor, block.T, lower=True).T


def small_solution(alphas, betas, block_width):
    steps_count = len(alphas)
    bidiagonal = jnp.zeros(
        ((steps_count + 1) * block_width, steps_count * block_width), jnp.float32
    )
    for position in range(steps_count):
        low = position * block_width
        bidiagonal = bidiagonal.at[low : low + block_width, low : low + block_width].set(
            alphas[position].T
        )
        bidiagonal = bidiagonal.at[
            low + block_width : low + 2 * block_width, low : low + block_width
        ].set(betas[position + 1])
    normal_matrix = product(bidiagonal.T, bidiagonal)
    target = jnp.zeros((steps_count * block_width, block_width), jnp.float32)
    target = target.at[:block_width].set(product(alphas[0], betas[0]))
    factor = jnp.linalg.cholesky(normal_matrix)
    return jax.scipy.linalg.cho_solve((factor, True), target)


def per_device(genotypes, right_sides, inverse_r):
    block_width = right_sides.shape[1]
    share_rows = right_sides.shape[0]

    def forward(direction):
        return product(inverse_r, lax.all_gather(direction, "cols", axis=0, tiled=True))

    lower_factor = jnp.linalg.cholesky(
        lax.psum(product(right_sides.T, right_sides), ("rows", "cols"))
    )
    betas = [lower_factor.T]
    basis_share = orthonormal(lower_factor, right_sides)
    basis_full = lax.all_gather(basis_share, "cols", axis=0, tiled=True)
    alphas = []
    directions = []
    for iteration in range(ITERS):
        partial_sums = product(genotypes.T, basis_full)
        summed = lax.psum(partial_sums, "rows")
        image = lax.psum_scatter(
            product(inverse_r.T, summed), "cols", scatter_dimension=0, tiled=True
        )
        if iteration > 0:
            image = image - product(directions[-1], betas[-1].T)
        lower_factor = jnp.linalg.cholesky(lax.psum(product(image.T, image), "cols"))
        alphas.append(lower_factor.T)
        directions.append(orthonormal(lower_factor, image))
        preconditioned = forward(directions[-1])
        mapped = lax.psum(product(genotypes, preconditioned), "cols") - product(
            basis_full, alphas[-1].T
        )
        lower_factor = jnp.linalg.cholesky(lax.psum(product(mapped.T, mapped), "rows"))
        betas.append(lower_factor.T)
        basis_full = orthonormal(lower_factor, mapped)
    basis_share = lax.dynamic_slice_in_dim(
        basis_full, lax.axis_index("cols") * share_rows, share_rows, 0
    )
    coefficients = small_solution(alphas, betas, block_width)
    combined = jnp.zeros(directions[0].shape, jnp.float32)
    for position in range(ITERS):
        combined = combined + product(
            directions[position],
            coefficients[position * block_width : (position + 1) * block_width],
        )
    return (forward(combined), basis_share)


def solution(mesh):
    in_specs = (P("rows", "cols"), P(("rows", "cols"), None), P("cols", None))
    out_specs = (P("cols", None), P(("rows", "cols"), None))
    return jax.shard_map(
        per_device, mesh=mesh, in_specs=in_specs, out_specs=out_specs, check_vma=False
    )
```

profile of v0, /device:TPU:1, one launch (start us, length us, event | category | flops | bytes accessed | tf_op | source)
XLA Modules:
  0.0 1156.2 jit_solution(632603851354833674)
XLA Ops:
  8.8 81.5 %psum.63 = f32[64,64]{0,1:T(8,128)S(1)} all-reduce(f32[64,64]{0,1:T(8,128)S(1)} %fusion.50), channel_id=1, replica_groups=mesh['rows'=32,'cols'=8] {'rows','cols'}, use_global_device_ids=true, to_apply=%region_0.0 | all-reduce | flops 4096 | bytes 32768 | tf_op jit(solution)/shard_map/psum | solution.py:45
  90.4 5.8 cholesky.124
  104.7 23.9 %all-gather.2.cloned.1.call-done = f32[9216,64]{0,1:T(8,128)} async-done(((f32[1152,64]{0,1:T(8,128)}), f32[9216,64]{0,1:T(8,128)}) %all-gather.2.cloned.1.call-update) | async-done | bytes 2359312 | tf_op jit(solution)/shard_map/all_gather | solution.py:49
  128.7 9.9 convolution_bitcast_fusion.7
  138.7 135.2 %all-reduce.7.cloned.1.call-done = f32[256,64]{0,1:T(8,128)} async-done(((f32[256,64]{0,1:T(8,128)}), f32[256,64]{0,1:T(8,128)}) %all-reduce.7.cloned.1.call-update) | async-done | bytes 65552 | tf_op jit(solution)/shard_map/psum | solution.py:54
  277.0 33.5 %reduce-scatter.3.cloned.1.call-done = f32[256,64]{0,1:T(8,128)} async-done(((f32[2048,64]{0,1:T(8,128)}), f32[256,64]{0,1:T(8,128)}) %reduce-scatter.3.cloned.1.call-update) | async-done | bytes 65552 | tf_op jit(solution)/shard_map/reduce_scatter | solution.py:55
  311.6 23.6 %psum.65 = f32[64,64]{0,1:T(8,128)S(1)} all-reduce(f32[64,64]{0,1:T(8,128)S(1)} %fusion.51), channel_id=1, replica_groups=mesh['rows'=32,'cols'=8] {'cols'}, use_global_device_ids=true, to_apply=%region_5.7 | all-reduce | flops 4096 | bytes 32768 | tf_op jit(solution)/shard_map/psum | solution.py:60
  335.3 5.8 cholesky.135
  348.5 16.7 %all_gather.13 = f32[2048,64]{0,1:T(8,128)S(1)} all-gather(f32[256,64]{0,1:T(8,128)S(1)} %bitcast.132), channel_id=1, replica_groups=mesh['rows'=32,'cols'=8] {'cols'}, dimensions={0}, use_global_device_ids=true | all-gather | bytes 589824 | tf_op jit(solution)/shard_map/all_gather | solution.py:42
  367.2 14.0 %convolution_bitcast_fusion.1 = f32[9216,64]{0,1:T(8,128)} fusion(f32[64,256]{1,0:T(8,128)S(1)} %fusion.52, f32[9216,256]{1,0:T(8,128)} %param.18), kind=kOutput, calls=%fused_computation.3 | convolution fusion | flops 1811939328 | bytes 11862016 | tf_op jit(solution)/shard_map/dot_general | solution.py:10
  381.8 68.5 %all-reduce.9.cloned.1.call-done = f32[9216,64]{0,1:T(8,128)} async-done(((f32[9216,64]{0,1:T(8,128)}), f32[9216,64]{0,1:T(8,128)}) %all-reduce.9.cloned.1.call-update) | async-done | bytes 2359312 | tf_op jit(solution)/shard_map/psum | solution.py:64
  458.3 115.4 %psum.67 = f32[64,64]{0,1:T(8,128)S(1)} all-reduce(f32[64,64]{0,1:T(8,128)S(1)} %fusion.53), channel_id=1, replica_groups=mesh['rows'=32,'cols'=8] {'rows'}, use_global_device_ids=true, to_apply=%region_7.10 | all-reduce | flops 4096 | bytes 32768 | tf_op jit(solution)/shard_map/psum | solution.py:67
  573.8 5.8 cholesky.146
  591.1 8.0 convolution_bitcast_fusion.6
  599.3 158.3 %all-reduce.11.cloned.1.call-done = f32[256,64]{0,1:T(8,128)} async-done(((f32[256,64]{0,1:T(8,128)}), f32[256,64]{0,1:T(8,128)}) %all-reduce.11.cloned.1.call-update) | async-done | bytes 65552 | tf_op jit(solution)/shard_map/psum | solution.py:54
  760.7 33.5 %reduce-scatter.5.cloned.1.call-done = f32[256,64]{0,1:T(8,128)} async-done(((f32[2048,64]{0,1:T(8,128)}), f32[256,64]{0,1:T(8,128)}) %reduce-scatter.5.cloned.1.call-update) | async-done | bytes 65552 | tf_op jit(solution)/shard_map/reduce_scatter | solution.py:55
  796.2 23.7 %psum.69 = f32[64,64]{0,1:T(8,128)S(1)} all-reduce(f32[64,64]{0,1:T(8,128)S(1)} %fusion.54), channel_id=1, replica_groups=mesh['rows'=32,'cols'=8] {'cols'}, use_global_device_ids=true, to_apply=%region_10.14 | all-reduce | flops 4096 | bytes 32768 | tf_op jit(solution)/shard_map/psum | solution.py:60
  832.3 16.5 %all_gather.14 = f32[2048,64]{0,1:T(8,128)S(1)} all-gather(f32[256,64]{0,1:T(8,128)S(1)} %bitcast.133), channel_id=1, replica_groups=mesh['rows'=32,'cols'=8] {'cols'}, dimensions={0}, use_global_device_ids=true | all-gather | bytes 589824 | tf_op jit(solution)/shard_map/all_gather | solution.py:42
  850.9 14.0 %convolution_bitcast_fusion = f32[9216,64]{0,1:T(8,128)} fusion(f32[64,256]{1,0:T(8,128)S(1)} %fusion.55, f32[9216,256]{1,0:T(8,128)} %param.18), kind=kOutput, calls=%fused_computation.1 | convolution fusion | flops 1811939328 | bytes 11862016 | tf_op jit(solution)/shard_map/dot_general | solution.py:10
  867.8 66.0 %all-reduce.13.cloned.1.call-done = f32[9216,64]{0,1:T(8,128)} async-done(((f32[9216,64]{0,1:T(8,128)}), f32[9216,64]{0,1:T(8,128)}) %all-reduce.13.cloned.1.call-update) | async-done | bytes 2359312 | tf_op jit(solution)/shard_map/psum | solution.py:64
  941.9 115.6 %psum.71 = f32[64,64]{0,1:T(8,128)S(1)} all-reduce(f32[64,64]{0,1:T(8,128)S(1)} %fusion.56), channel_id=1, replica_groups=mesh['rows'=32,'cols'=8] {'rows'}, use_global_device_ids=true, to_apply=%region_12.16 | all-reduce | flops 4096 | bytes 32768 | tf_op jit(solution)/shard_map/psum | solution.py:67
  1076.4 11.7 %cholesky.41 = f32[128,128]{1,0:T(8,128)S(1)} custom-call(f32[128,128]{1,0:T(8,128)S(1)} %fusion.9), custom_call_target="Cholesky" | custom-call | tf_op jit(solution)/shard_map/jit(cholesky)/cholesky | solution.py:33
  1089.5 9.8 custom-call.23
  1100.7 44.0 %all_gather.15 = f32[2048,64]{1,0:T(8,128)S(1)} all-gather(f32[256,64]{1,0:T(8,128)S(1)} %convolution_add_fusion), channel_id=1, replica_groups=mesh['rows'=32,'cols'=8] {'cols'}, dimensions={0}, use_global_device_ids=true | all-gather | bytes 589824 | tf_op jit(solution)/shard_map/all_gather | solution.py:42
  (90 shorter events, 100.2 us)
Async XLA Ops:
  7.2 266.8 %copy-start = (f32[256,2048]{1,0:T(8,128)S(1)}, f32[256,2048]{1,0:T(8,128)}, u32[]{:S(2)}) copy-start(f32[256,2048]{1,0:T(8,128)} %param.20) | copy-start | bytes 6291460
  7.2 121.5 %all-gather.2.cloned.1.call-start = ((), (), s32[]{:S(2)}) async-start(), calls=%async_computation.2 | async-start | bytes 2654208 | tf_op jit(solution)/shard_map/all_gather | solution.py:49
  104.7 169.2 %all-reduce.7.cloned.1.call-start = ((), (), s32[]{:S(2)}) async-start(), calls=%async_computation.3 | async-start | bytes 131072 | tf_op jit(solution)/shard_map/psum | solution.py:54
  138.6 171.9 %reduce-scatter.3.cloned.1.call-start = ((), (), s32[]{:S(2)}) async-start(), calls=%async_computation.4 | async-start | bytes 589824 | tf_op jit(solution)/shard_map/reduce_scatter | solution.py:55
  277.0 173.3 %all-reduce.9.cloned.1.call-start = ((), (), s32[]{:S(2)}) async-start(), calls=%async_computation.5 | async-start | bytes 4718592 | tf_op jit(solution)/shard_map/psum | solution.py:64
  381.3 376.3 %all-reduce.11.cloned.1.call-start = ((), (), s32[]{:S(2)}) async-start(), calls=%async_computation.6 | async-start | bytes 131072 | tf_op jit(solution)/shard_map/psum | solution.py:54
  454.9 1.4 copy-start.2
  589.7 1.4 copy-start.3
  599.2 195.0 %reduce-scatter.5.cloned.1.call-start = ((), (), s32[]{:S(2)}) async-start(), calls=%async_computation.7 | async-start | bytes 589824 | tf_op jit(solution)/shard_map/reduce_scatter | solution.py:55
  760.6 173.2 %all-reduce.13.cloned.1.call-start = ((), (), s32[]{:S(2)}) async-start(), calls=%async_computation.8 | async-start | bytes 4718592 | tf_op jit(solution)/shard_map/psum | solution.py:64
  938.4 1.4 copy-start.1
Sparse Core Ops, SparseCore 0:
  104.8 23.8 all-gather.1
  138.7 135.1 all-reduce.6
  277.1 33.3 reduce-scatter.2
  381.4 68.8 all-reduce.8
  599.3 158.2 all-reduce.10
  760.8 33.3 reduce-scatter.4
  865.0 68.7 all-reduce.12
where the time goes:
time: 1170 us; the launch traced here: 1160 us
  waiting for transfers between devices  519 us (44%)
  blocking collectives  437 us (37%)
  matrix products  91.7 us (8%)
  other arithmetic  83.3 us (7%)
  between operations  14.9 us (1%)
    psum x2, waiting for transfers between devices, per_device(): summed = lax.psum(partial_sums, 'rows')  294 us
    psum x2, blocking collectives, per_device(): lax.psum(product(mapped.T, mapped), 'rows')  231 us
    psum x2, waiting for transfers between devices, per_device(): lax.psum(product(genotypes, preconditioned), 'cols')  134 us
    psum x1, blocking collectives, per_device(): lax.psum(product(right_sides.T, right_sides), ('rows', 'cols'))  81.5 us
    dot_general x21, matrix products, product(): jnp.dot(left, right, precision=lax.Precision.HIGHEST, preferred_element_t...  78.7 us
    all_gather x3, blocking collectives, forward(): lax.all_gather(direction, 'cols', axis=0, tiled=True)  77.2 us
    reduce_scatter x2, waiting for transfers between devices, per_device(): lax.psum_scatter(product(inverse_r.T, summed), 'cols', scatter_dimension=...  67 us
    psum x2, blocking collectives, per_device(): lax.psum(product(image.T, image), 'cols')  47.3 us
  transfers between devices with their start and end apart: 7, of which 7 were waited for; matrix products, arithmetic and copies ran while one was open for 0% of the time, Pallas kernels for 0%

commit v1 on v0

v1 whole, which is shorter than its diff:
```python
import functools

import jax
import jax.numpy as jnp
from jax import lax
from jax.experimental import pallas as pl
from jax.experimental.pallas import tpu as pltpu
from jax.sharding import PartitionSpec as P

F32 = jnp.float32
BF16 = jnp.bfloat16
NN = (((1,), (0,)), ((), ()))
NT = (((1,), (1,)), ((), ()))
CHIPS = 4
CORES = 2
PEERS = CHIPS * CORES
SCALE = 4096.0


def exact(left, right, dims=NN):
    return lax.dot_general(
        left, right, dims, precision=lax.Precision.HIGHEST, preferred_element_type=F32
    )


def parts(value):
    high = value.astype(BF16)
    return high, (value - high.astype(F32)).astype(BF16)


def three_pass(value, high, low, dims):
    rows = value.shape[0]
    v_high, v_low = parts(value)
    both = lax.dot_general(
        jnp.concatenate([v_high, v_low], axis=0), high, dims, preferred_element_type=F32
    )
    return (
        both[:rows]
        + both[rows:]
        + lax.dot_general(v_high, low, dims, preferred_element_type=F32)
    )


def doubled(rows):
    return jnp.concatenate([rows, rows], axis=0)


def iotas(size):
    row = lax.broadcasted_iota(jnp.int32, (size, 2 * size), 0)
    lane = lax.broadcasted_iota(jnp.int32, (size, 2 * size), 1)
    return row, lane


def with_identity(twice):
    size = twice.shape[0]
    row, lane = iotas(size)
    return jnp.where(lane < size, jnp.where(lane == row, 1.0, 0.0), twice)


def eliminate(systems, full):
    size = systems[0].shape[0]
    row_at, _ = iotas(size)
    systems = list(systems)
    for j in range(size):
        for i, m in enumerate(systems):
            column = m[:, size + j : size + j + 1]
            row = m[j : j + 1, :] * (1.0 / m[j : j + 1, size + j : size + j + 1])
            if full[i]:
                systems[i] = jnp.where(row_at == j, row, m - column * row)
            else:
                systems[i] = jnp.where(row_at > j, m - column * row, m)
    return systems


def inverse(twice):
    size = twice.shape[0]
    return eliminate([with_identity(twice)], [True])[0][:, :size]


def diagonal(twice):
    size = twice.shape[0]
    row, lane = iotas(size)
    as_column = jnp.sum(jnp.where(lane == row, twice, 0.0), axis=1, keepdims=True)
    hit = jnp.logical_or(lane == row, lane == row + size)
    as_row = jnp.sum(jnp.where(hit, twice, 0.0), axis=0, keepdims=True)
    return as_column, as_row


class Net:
    def __init__(self, send_sems, recv_sems):
        self.send_sems, self.recv_sems = send_sems, recv_sems
        self.sent = []

    def send(self, source, target, **device):
        at = len(self.sent)
        copy = pltpu.make_async_remote_copy(
            src_ref=source,
            dst_ref=target,
            send_sem=self.send_sems.at[at],
            recv_sem=self.recv_sems.at[at],
            device_id=device,
            device_id_type=pl.DeviceIdType.MESH,
        )
        copy.start()
        self.sent.append(copy)
        return copy

    def finish(self):
        for copy in self.sent:
            copy.wait_send()


def body(
    nz, ny,
    g_hbm, b_ref, p_ref, u_ref, s_ref,
    g_f32, g_high, g_low, p_high, p_low,
    b_full, n_full, i_full, j_full, j_out,
    y_part, y_sib, y_fwd, y_left, y_right,
    t_part, t_sib, t_fwd, t_left, t_right,
    az, zbuf, ybuf,
    sm_own, sm_x, sm_z, sm_y, sm_out,
    g_sems, send_sems, recv_sems,
):
    width, rows_w = b_ref.shape
    block = p_ref.shape[0]
    half = width // 2
    r, c = lax.axis_index("rows"), lax.axis_index("cols")
    x, k = c // CORES, c % CORES
    z, y = r // ny, r % ny
    right = lax.rem(x + 1, CHIPS)
    left = lax.rem(x + CHIPS - 1, CHIPS)
    opposite = lax.rem(x + 2, CHIPS)
    c_sib = x * CORES + 1 - k
    c_right, c_left, c_opp = (chip * CORES + k for chip in (right, left, opposite))
    net = Net(send_sems, recv_sems)

    def chunk(at):
        return pl.ds(pl.multiple_of(at * rows_w, rows_w), rows_w)

    loads = []
    for step, at in enumerate((c, c_sib, c_left, c_right, c_left + 1 - 2 * k, c_right + 1 - 2 * k, c_opp, c_opp + 1 - 2 * k)):
        copy = pltpu.make_async_copy(g_hbm.at[chunk(at)], g_f32.at[chunk(at)], g_sems.at[step])
        copy.start()
        loads.append(copy)

    barrier = pltpu.get_barrier_semaphore()
    greeted = 0
    for d in range(1, PEERS):
        pl.semaphore_signal(barrier, inc=1, device_id={"cols": lax.rem(c + d, PEERS)}, device_id_type=pl.DeviceIdType.MESH)
        greeted += 1
    for d in range(1, nz):
        pl.semaphore_signal(barrier, inc=1, device_id={"rows": lax.rem(z + d, nz) * ny + y}, device_id_type=pl.DeviceIdType.MESH)
        greeted += 1
    for d in range(1, ny):
        pl.semaphore_signal(barrier, inc=1, device_id={"rows": z * ny + lax.rem(y + d, ny)}, device_id_type=pl.DeviceIdType.MESH)
        greeted += 1
    b_full[c] = b_ref[...]
    pl.semaphore_wait(barrier, greeted)

    upper, lower = pl.ds(0, half), pl.ds(half, half)

    def gather(full, on_block):
        def copy_to(at, rows, target):
            return net.send(full.at[at, rows], full.at[at, rows], cols=target)

        right_upper = copy_to(c, upper, c_right)
        left_lower = copy_to(c, lower, c_left)
        right_lower = copy_to(c, lower, c_right)
        left_upper = copy_to(c, upper, c_left)
        sib_own = net.send(full.at[c], full.at[c], cols=c_sib)
        on_block(c, 0)
        right_upper.wait_recv()
        onward_right = copy_to(c_left, upper, c_right)
        sib_left_upper = copy_to(c_left, upper, c_sib)
        left_lower.wait_recv()
        onward_left = copy_to(c_right, lower, c_left)
        sib_right_lower = copy_to(c_right, lower, c_sib)
        sib_own.wait_recv()
        on_block(c_sib, 1)
        right_lower.wait_recv()
        sib_left_lower = copy_to(c_left, lower, c_sib)
        left_upper.wait_recv()
        sib_right_upper = copy_to(c_right, upper, c_sib)
        on_block(c_left, 2)
        on_block(c_right, 3)
        sib_left_upper.wait_recv()
        sib_left_lower.wait_recv()
        on_block(c_left + 1 - 2 * k, 4)
        sib_right_lower.wait_recv()
        sib_right_upper.wait_recv()
        on_block(c_right + 1 - 2 * k, 5)
        onward_right.wait_recv()
        sib_opp_upper = copy_to(c_opp, upper, c_sib)
        onward_left.wait_recv()
        sib_opp_lower = copy_to(c_opp, lower, c_sib)
        on_block(c_opp, 6)
        sib_opp_upper.wait_recv()
        sib_opp_lower.wait_recv()
        on_block(c_opp + 1 - 2 * k, 7)

    def scatter(compute, part, sib, fwd, from_left, from_right, beside=None):
        def pair(chip, slot):
            mine, theirs = chip * CORES + k, chip * CORES + 1 - k
            part[theirs] = compute(theirs)
            copy = net.send(part.at[theirs], sib.at[slot], cols=c_sib)
            part[mine] = compute(mine)
            return copy

        sib_opp = pair(opposite, 0)
        sib_right = pair(right, 1)
        sib_opp.wait_recv()
        part[c_opp] = part[c_opp] + sib[0]
        fwd_upper = net.send(part.at[c_opp, upper], fwd.at[upper], cols=c_right)
        fwd_lower = net.send(part.at[c_opp, lower], fwd.at[lower], cols=c_left)
        sib_left = pair(left, 2)
        sib_right.wait_recv()
        part[c_right] = part[c_right] + sib[1]
        right_lower = net.send(part.at[c_right, lower], from_left.at[lower], cols=c_right)
        sib_own = pair(x, 3)
        sib_left.wait_recv()
        part[c_left] = part[c_left] + sib[2]
        left_upper = net.send(part.at[c_left, upper], from_right.at[upper], cols=c_left)
        fwd_upper.wait_recv()
        part[c_right, upper] = part[c_right, upper] + fwd[upper]
        right_upper = net.send(part.at[c_right, upper], from_left.at[upper], cols=c_right)
        fwd_lower.wait_recv()
        part[c_left, lower] = part[c_left, lower] + fwd[lower]
        left_lower = net.send(part.at[c_left, lower], from_right.at[lower], cols=c_left)
        extra = beside() if beside is not None else None
        sib_own.wait_recv()
        total = part[c] + sib[3]
        for copy in (right_lower, left_upper, right_upper, left_lower):
            copy.wait_recv()
        return total + from_left[...] + from_right[...], extra

    share = width // nz

    def sum_rows(value, at, full):
        own, zb, yb = az.at[at], zbuf.at[at], ybuf.at[at]
        own[...] = value
        copies = []
        for d in range(1, nz):
            to = lax.rem(z + d, nz)
            copies.append(net.send(own.at[pl.ds(pl.multiple_of(to * share, share), share)], zb.at[d - 1], rows=to * ny + y))
        mine = pl.ds(pl.multiple_of(z * share, share), share)
        total = own[mine]
        for d in range(1, nz):
            copies[d - 1].wait_recv()
            total = total + zb[d - 1]
        yb[y] = total
        copies = [
            net.send(yb.at[y], yb.at[y], rows=z * ny + lax.rem(y + d, ny)) for d in range(1, ny)
        ]
        for copy in copies:
            copy.wait_recv()
        total = yb[0]
        for i in range(1, ny):
            total = total + yb[i]
        full[c, mine] = total
        copies = [
            net.send(full.at[c, mine], full.at[c, mine], rows=lax.rem(z + d, nz) * ny + y) for d in range(1, nz)
        ]
        for copy in copies:
            copy.wait_recv()

    def small_sum(value, at):
        piece = width // PEERS
        own, xb, zb, yb, out = sm_own.at[at], sm_x.at[at], sm_z.at[at], sm_y.at[at], sm_out.at[at]
        own[...] = value
        copies = []
        for d in range(1, PEERS):
            to = lax.rem(c + d, PEERS)
            copies.append(net.send(own.at[pl.ds(pl.multiple_of(to * piece, piece), piece)], xb.at[d - 1], cols=to))
        yield
        mine = pl.ds(pl.multiple_of(c * piece, piece), piece)
        total = own[mine]
        for d in range(1, PEERS):
            copies[d - 1].wait_recv()
            total = total + xb[d - 1]
        zb[z] = total
        copies = [
            net.send(zb.at[z], zb.at[z], rows=lax.rem(z + d, nz) * ny + y) for d in range(1, nz)
        ]
        yield
        for copy in copies:
            copy.wait_recv()
        total = zb[0]
        for i in range(1, nz):
            total = total + zb[i]
        yb[y] = total
        copies = [
            net.send(yb.at[y], yb.at[y], rows=z * ny + lax.rem(y + d, ny)) for d in range(1, ny)
        ]
        yield
        for copy in copies:
            copy.wait_recv()
        total = yb[0]
        for i in range(1, ny):
            total = total + yb[i]
        out[mine] = total
        copies = [
            net.send(out.at[mine], out.at[mine], cols=lax.rem(c + d, PEERS)) for d in range(1, PEERS)
        ]
        yield
        for copy in copies:
            copy.wait_recv()
        yield

    def backward(full, first=None):
        totals = [None]

        def on_block(at, step):
            if first is not None:
                first(at, step)
            term = three_pass(full[at], g_high[chunk(at)], g_low[chunk(at)], NN)
            totals[0] = term if totals[0] is None else totals[0] + term

        gather(full, on_block)
        return totals[0]

    def transpose_applied(value, at, full):
        def compute(j):
            lanes = pl.ds(pl.multiple_of(j * block, block), block)
            return three_pass(value, p_high[:, lanes], p_low[:, lanes], NN)

        total, _ = scatter(compute, t_part.at[at], t_sib.at[at], t_fwd.at[at], t_left.at[at], t_right.at[at])
        sum_rows(total, at, full)
        gather(full, lambda *_: None)

    def applied(full):
        total = None
        for j in range(PEERS):
            lanes = pl.ds(j * block, block)
            term = three_pass(full[j], p_high[:, lanes], p_low[:, lanes], NT)
            total = term if total is None else total + term
        return total

    def forward(value, at, beside):
        def compute(j):
            return three_pass(value, g_high[chunk(j)], g_low[chunk(j)], NT)

        return scatter(compute, y_part.at[at], y_sib.at[at], y_fwd.at[at], y_left.at[at], y_right.at[at], beside)

    def gram(left, right):
        total = None
        for j in range(PEERS):
            term = exact(left[j], doubled(right[j]), NT)
            total = term if total is None else total + term
        return total

    b_own = b_ref[...]
    sums = small_sum(exact(b_own, doubled(b_own), NT), 0)

    def load(at, step):
        loads[step].wait()
        high, low = parts(g_f32[chunk(at)])
        g_high[chunk(at)] = high
        g_low[chunk(at)] = low
        if step in (0, 1, 3, 5, 6):
            next(sums)

    p_high[...], p_low[...] = parts(p_ref[...])
    summed = backward(b_full, load)
    transpose_applied(summed, 0, i_full)
    x_one = applied(i_full)

    def beside_one():
        c_zero = gram(i_full, i_full)
        return c_zero, inverse(sm_out[0])

    y_one, (c_zero, gram_inverse) = forward(x_one, 0, beside_one)
    scale_one, scale_one_row = (lax.rsqrt(v) for v in diagonal(c_zero))
    c_one = c_zero[:, :width]
    left_one = exact(c_one, gram_inverse)
    n_one = scale_one * (y_one - exact(left_one, b_own))
    n_full[c] = n_one

    summed = backward(n_full)
    c_inverse = inverse(c_zero)
    transpose_applied(summed, 1, j_full)
    x_jay = applied(j_full)
    h_raw = gram(j_full, i_full)
    out_of = exact(h_raw[:, :width], c_inverse)
    x_two = x_jay - exact(out_of, x_one)

    def beside_two():
        for j in range(PEERS):
            j_out[j] = j_full[j] - exact(out_of, i_full[j])
        e_raw = gram(j_out, j_out)
        scale_two, scale_two_row = (lax.rsqrt(v) for v in diagonal(e_raw))
        h_one = h_raw * scale_one_row
        c_row = c_zero * scale_one_row
        normal = h_one + scale_one * exact(left_one, c_row)
        h_inv, s_inv = (
            m[:, :width]
            for m in eliminate([with_identity(h_one), with_identity(normal)], [True, True])
        )
        e_col = scale_two * e_raw[:, :width]
        e_row = e_raw * scale_two_row
        schur = exact(exact(e_col, h_inv - s_inv), e_row)
        d_t = exact(c_row[:, :width], s_inv)
        w = exact(d_t, e_row[:, :width])
        back = exact(exact(e_raw[:, :width], h_inv), n_one)
        return scale_two, e_col, c_row, s_inv, schur, w, back

    y_two, (scale_two, e_col, c_row, s_inv, schur, w, back) = forward(x_two, 1, beside_two)
    n_two = scale_two * (y_two - back)
    for _ in small_sum(exact(n_two, doubled(n_two), NT), 1):
        pass
    h_two = sm_out[1]
    lower_inv, last = eliminate(
        [with_identity(h_two), with_identity(h_two + schur)], [False, True]
    )
    row_at, lane_at = iotas(width)
    pivots = jnp.sum(jnp.where(lane_at == row_at + width, lower_inv, 0.0), axis=1, keepdims=True)
    u_ref[...] = exact(lax.rsqrt(pivots) * lower_inv[:, :width], n_two)
    b_t = -exact(w, last[:, :width])
    a_t = exact(c_row[:, :width] - exact(b_t, e_col), s_inv)
    s_ref[...] = SCALE * (exact(a_t, scale_one * x_one) + exact(b_t, scale_two * x_two))
    net.finish()


def solution(mesh, ny=4):
    nrows = mesh.shape["rows"]
    nz = nrows // ny

    def per_device(genotypes, right_sides, inverse_r):
        rows, block = genotypes.shape
        rows_w, width = right_sides.shape
        variants = inverse_r.shape[1]
        share = width // nz
        piece = width // PEERS
        v = pltpu.VMEM
        messages = 4 * 13 + 4 * 10 + 2 * (2 * (nz - 1) + ny - 1) + 2 * (2 * (PEERS - 1) + nz + ny - 2)
        u_t, s_t = pl.pallas_call(
            functools.partial(body, nz, ny),
            out_shape=(
                jax.ShapeDtypeStruct((width, rows_w), F32),
                jax.ShapeDtypeStruct((width, block), F32),
            ),
            in_specs=[
                pl.BlockSpec(memory_space=pl.ANY),
                pl.BlockSpec(memory_space=pltpu.VMEM),
                pl.BlockSpec(memory_space=pltpu.VMEM),
            ],
            out_specs=[pl.BlockSpec(memory_space=pltpu.VMEM)] * 2,
            scratch_shapes=[
                v((rows, block), F32), v((rows, block), BF16), v((rows, block), BF16),
                v((block, variants), BF16), v((block, variants), BF16),
                v((PEERS, width, rows_w), F32), v((PEERS, width, rows_w), F32),
                v((PEERS, width, block), F32), v((PEERS, width, block), F32), v((PEERS, width, block), F32),
                v((2, PEERS, width, rows_w), F32), v((2, CHIPS, width, rows_w), F32),
                v((2, width, rows_w), F32), v((2, width, rows_w), F32), v((2, width, rows_w), F32),
                v((2, PEERS, width, block), F32), v((2, CHIPS, width, block), F32),
                v((2, width, block), F32), v((2, width, block), F32), v((2, width, block), F32),
                v((2, width, block), F32), v((2, nz - 1, share, block), F32), v((2, ny, share, block), F32),
                v((2, width, 2 * width), F32), v((2, PEERS - 1, piece, 2 * width), F32),
                v((2, nz, piece, 2 * width), F32), v((2, ny, piece, 2 * width), F32),
                v((2, width, 2 * width), F32),
                pltpu.SemaphoreType.DMA((PEERS,)),
                pltpu.SemaphoreType.DMA((messages,)),
                pltpu.SemaphoreType.DMA((messages,)),
            ],
            compiler_params=pltpu.CompilerParams(
                collective_id=0, has_side_effects=True, vmem_limit_bytes=58 * 1024 * 1024
            ),
        )(genotypes, right_sides.T * (1.0 / SCALE), inverse_r)
        return s_t.T, u_t.T

    in_specs = (P("rows", "cols"), P(("rows", "cols"), None), P("cols", None))
    out_specs = (P("cols", None), P(("rows", "cols"), None))
    return jax.shard_map(
        per_device, mesh=mesh, in_specs=in_specs, out_specs=out_specs, check_vma=False
    )
```

time: 1170 us -> 182 us (0.16); the launches traced: 1160 us -> 181 us
  waiting for transfers between devices: 519 us -> 0 us
  blocking collectives: 437 us -> 0 us
  Pallas kernels: 0 us -> 176 us
  matrix products: 91.7 us -> 0 us
  other arithmetic: 83.3 us -> 1.7 us
  between operations: 14.9 us -> 0.64 us
    psum x4 -> x0, waiting for transfers between devices: 428 us -> none  [the longest x2 294 us: per_device(): summed = lax.psum(partial_sums, 'rows')]
    psum x5 -> x0, blocking collectives: 360 us -> none  [the longest x2 231 us: per_device(): lax.psum(product(mapped.T, mapped), 'rows')]
    pallas_call x0 -> x1, Pallas kernels: none -> 176 us  [per_device(): pl.pallas_call(functools.partial(body, nz, ny), out_shape=(jax.ShapeDtype...]
    another operation x30 -> x0, other arithmetic: 83.2 us -> none  [the longest x10 27.7 us: orthonormal(): jax.scipy.linalg.solve_triangular(lower_factor, block.T, lower=True)]
    dot_general x21 -> x0, matrix products: 78.7 us -> none  [product(): jnp.dot(left, right, precision=lax.Precision.HIGHEST, preferred_element_t...]
    all_gather x3 -> x0, blocking collectives: 77.2 us -> none  [forward(): lax.all_gather(direction, 'cols', axis=0, tiled=True)]
    reduce_scatter x2 -> x0, waiting for transfers between devices: 67 us -> none  [per_device(): lax.psum_scatter(product(inverse_r.T, summed), 'cols', scatter_dimension=...]
    all_gather x1 -> x0, waiting for transfers between devices: 23.9 us -> none  [per_device(): basis_full = lax.all_gather(basis_share, 'cols', axis=0, tiled=True)]
  transfers between devices with their start and end apart: 7 -> 0, of which waited for: 7 -> 0; matrix products, arithmetic and copies ran while one was open for 0% -> 0% of each run, Pallas kernels for 0% -> 0%
where the time goes in v1:
time: 182 us; the launch traced here: 181 us
  Pallas kernels  176 us (97%)
  local copies, waits for them, and re-layouts  3.17 us (2%)
    pallas_call x1, Pallas kernels, per_device(): pl.pallas_call(functools.partial(body, nz, ny), out_shape=(jax.ShapeDtype...  176 us

profile of v1, /device:TPU:1, one launch (start us, length us, event | category | flops | bytes accessed | tf_op | source)
XLA Modules:
  0.0 181.3 jit_solution(15570724604811154177)
XLA Ops:
  0.6 1.7 multiply_bitcast_fusion.b_ref
  2.3 175.8 %shard_map.50 = (f32[64,1152]{1,0:T(8,128)}, f32[64,256]{1,0:T(8,128)}) custom-call(f32[9216,256]{1,0:T(8,128)} %g_hbm.1, f32[64,1152]{1,0:T(8,128)} %multiply_bitcast_fusion.b_ref, f32[256,2048]{1,0:T(8,128)} %p_ref.1), custom_call_target="tpu_custom_call" | custom-call | tf_op jit(solution)/shard_map/pallas_call | solution.py:435
  178.2 1.5 copy.7
  179.6 1.7 copy.8

commit v2 on v1

v2 whole, which is shorter than its diff:
```python
import functools

import jax
import jax.numpy as jnp
from jax import lax
from jax.experimental import pallas as pl
from jax.experimental.pallas import tpu as pltpu
from jax.sharding import PartitionSpec as P

F32 = jnp.float32
BF16 = jnp.bfloat16
NN = (((1,), (0,)), ((), ()))
NT = (((1,), (1,)), ((), ()))
CHIPS = 4
CORES = 2
PEERS = CHIPS * CORES
SCALE = 4096.0


def exact(left, right, dims=NN):
    return lax.dot_general(
        left, right, dims, precision=lax.Precision.HIGHEST, preferred_element_type=F32
    )


def dot(left, right, dims):
    return lax.dot_general(left, right, dims, preferred_element_type=F32)


def parts(value):
    high = value.astype(BF16).astype(F32)
    rest = value - high
    middle = rest.astype(BF16).astype(F32)
    return high, middle, rest - middle


def stacked_parts(value):
    rows = value.shape[0]
    stack = jnp.concatenate(parts(value), axis=0)
    if 3 * rows % 16:
        stack = jnp.concatenate([stack, jnp.zeros((16 - 3 * rows % 16, value.shape[1]), F32)], axis=0)
    return stack.astype(BF16)


def with_counts(value, counts, dims):
    rows = value.shape[0]
    out = dot(stacked_parts(value), counts, dims)
    return out[2 * rows : 3 * rows] + out[rows : 2 * rows] + out[:rows]


def with_parts(value, right, dims):
    rows = value.shape[0]
    stack = stacked_parts(value)
    first = dot(stack, right[0], dims)
    second = dot(stack[: max(2 * rows, 16)], right[1], dims)
    small = first[2 * rows : 3 * rows] + second[rows : 2 * rows]
    return small + (first[rows : 2 * rows] + second[:rows]) + first[:rows]


def doubled(rows):
    return jnp.concatenate([rows, rows], axis=0)


def iotas(rows, lanes):
    row = lax.broadcasted_iota(jnp.int32, (rows, lanes), 0)
    lane = lax.broadcasted_iota(jnp.int32, (rows, lanes), 1)
    return row, lane


def with_identity(twice):
    size = twice.shape[0]
    row, lane = iotas(size, 2 * size)
    return jnp.where(lane < size, jnp.where(lane == row, 1.0, 0.0), twice)


def eliminate(systems, full, done, stride=4):
    size = systems[0].shape[0]
    shape = (size, 2 * size)
    row_at, _ = iotas(*shape)
    systems = list(systems)
    for j in range(0, size, 2):
        for i, m in enumerate(systems):
            first = jnp.broadcast_to(m[:, size + j : size + j + 1], shape)
            second = jnp.broadcast_to(m[:, size + j + 1 : size + j + 2], shape)
            top, bottom = m[j : j + 1, :], m[j + 1 : j + 2, :]
            inverse = 1.0 / first[j : j + 1, :]
            ratio = first[j + 1 : j + 2, :] * inverse
            across = second[j : j + 1, :]
            pivot = 1.0 / (second[j + 1 : j + 2, :] - ratio * across)
            row_two = (bottom - ratio * top) * pivot
            row_one = (top - across * row_two) * inverse
            less = m - first * row_one - second * row_two
            if full[i]:
                systems[i] = jnp.where(row_at == j, row_one, jnp.where(row_at == j + 1, row_two, less))
            else:
                systems[i] = jnp.where(row_at > j + 1, less, m)
        if j // 2 % stride == stride - 1:
            yield
    done.extend(systems)


def factors(m):
    size = m.shape[0]
    row, lane = iotas(size, 2 * size)
    odd = lax.rem(row, 2) == 1
    above = pltpu.roll(m, 1, 0)
    left = jnp.logical_and(odd, lane == row + size - 1)
    under = jnp.sum(jnp.where(left, m, 0.0), axis=1, keepdims=True)
    over = jnp.sum(jnp.where(left, above, jnp.where(jnp.logical_and(lane == 0, jnp.logical_not(odd)), 1.0, 0.0)), axis=1, keepdims=True)
    m = m - (under / over) * above
    pivots = jnp.sum(jnp.where(lane == row + size, m, 0.0), axis=1, keepdims=True)
    scaled = lax.rsqrt(pivots) * m
    upper = pltpu.roll(jnp.where(lane >= row + size, scaled, 0.0), size, 1)
    return scaled[:, :size], upper[:, :size]


def packed(twice):
    half = twice.shape[0] // 2
    _, lane = iotas(half, twice.shape[1])
    return jnp.where(lane < twice.shape[1] // 2, twice[:half], twice[half:])


def unpacked(pack):
    half, lanes = pack.shape
    _, lane = iotas(half, lanes)
    other = pltpu.roll(pack, lanes // 2, 1)
    first = lane < lanes // 2
    return jnp.concatenate([jnp.where(first, pack, other), jnp.where(first, other, pack)], axis=0)


class Net:
    def __init__(self, send_sems, recv_sems):
        self.send_sems, self.recv_sems = send_sems, recv_sems
        self.sent = []

    def send(self, source, target, **device):
        at = len(self.sent)
        copy = pltpu.make_async_remote_copy(
            src_ref=source,
            dst_ref=target,
            send_sem=self.send_sems.at[at],
            recv_sem=self.recv_sems.at[at],
            device_id=device,
            device_id_type=pl.DeviceIdType.MESH,
        )
        copy.start()
        self.sent.append(copy)
        return copy

    def finish(self):
        for copy in self.sent:
            copy.wait_send()


def body(
    nz, ny,
    g_hbm, b_hbm, p_hbm, n_ref, x_ref, m_ref,
    g_f32, b_own, p_f32, counts, lowest, spread, p_high, p_low,
    b_full, n_full, u_one,
    y_part, y_sib, y_fwd, y_left, y_right,
    az, y_in, z_in, t_out, t_in, i_all, z_all, x_all,
    c_in, sm_own, sm_x, sm_z, sm_y, sm_out,
    g_sems, send_sems, recv_sems,
):
    width, rows_w = b_own.shape
    block = p_f32.shape[0]
    half = width // 2
    quarter = width // 4
    r, c = lax.axis_index("rows"), lax.axis_index("cols")
    x, k = c // CORES, c % CORES
    z, y = r // ny, r % ny
    right = lax.rem(x + 1, CHIPS)
    left = lax.rem(x + CHIPS - 1, CHIPS)
    opposite = lax.rem(x + 2, CHIPS)
    c_sib = x * CORES + 1 - k
    c_right, c_left, c_opp = (chip * CORES + k for chip in (right, left, opposite))
    net = Net(send_sems, recv_sems)

    def chunk(at):
        return pl.ds(pl.multiple_of(at * rows_w, rows_w), rows_w)

    def c_peer(d):
        return lax.rem(c + d, PEERS)

    def z_peer(d):
        return lax.rem(z + d, nz) * ny + y

    def y_peer(d):
        return z * ny + lax.rem(y + d, ny)

    barrier = pltpu.get_barrier_semaphore()
    greeted = [{"rows": z_peer(d)} for d in range(1, nz)]
    greeted += [{"rows": y_peer(d)} for d in range(1, ny)]
    greeted += [{"cols": c_peer(d)} for d in range(1, PEERS)]
    for device in greeted:
        pl.semaphore_signal(barrier, inc=1, device_id=device, device_id_type=pl.DeviceIdType.MESH)

    own_load = pltpu.make_async_copy(b_hbm, b_own, g_sems.at[PEERS])
    p_load = pltpu.make_async_copy(p_hbm, p_f32, g_sems.at[PEERS + 1])
    own_load.start()
    loads = []
    for step, at in enumerate((c, c_sib, c_left, c_right, c_left + 1 - 2 * k, c_right + 1 - 2 * k, c_opp, c_opp + 1 - 2 * k)):
        copy = pltpu.make_async_copy(g_hbm.at[chunk(at)], g_f32.at[chunk(at)], g_sems.at[step])
        copy.start()
        loads.append(copy)
    p_load.start()
    own_load.wait()
    b_own[...] = b_own[...] * (1.0 / SCALE)
    b_full[c] = b_own[...]
    b_gram = exact(b_own[...], doubled(b_own[...]), NT)
    p_load.wait()
    p_high[...], p_low[...] = (v.astype(BF16) for v in parts(p_f32[...])[:2])
    pl.semaphore_wait(barrier, len(greeted))

    work = [iter(())]

    def fill(pieces):
        for _ in range(pieces):
            next(work[0], None)

    def finish(steps):
        for _ in steps:
            pass

    def half_rows(h):
        return (
            pl.ds(h * half, half),
            pl.ds(h * half, quarter),
            pl.ds(h * half + quarter, quarter),
        )

    def gather(full, h, on_block):
        rows, upper, lower = half_rows(h)

        def copy_to(at, rows, target):
            return net.send(full.at[at, rows], full.at[at, rows], cols=target)

        right_upper = copy_to(c, upper, c_right)
        left_lower = copy_to(c, lower, c_left)
        yield
        right_lower = copy_to(c, lower, c_right)
        left_upper = copy_to(c, upper, c_left)
        sib_own = copy_to(c, rows, c_sib)
        yield
        on_block(c, 0)
        right_upper.wait_recv()
        onward_right = copy_to(c_left, upper, c_right)
        sib_left_upper = copy_to(c_left, upper, c_sib)
        left_lower.wait_recv()
        onward_left = copy_to(c_right, lower, c_left)
        sib_right_lower = copy_to(c_right, lower, c_sib)
        yield
        sib_own.wait_recv()
        on_block(c_sib, 1)
        right_lower.wait_recv()
        sib_left_lower = copy_to(c_left, lower, c_sib)
        left_upper.wait_recv()
        sib_right_upper = copy_to(c_right, upper, c_sib)
        on_block(c_left, 2)
        on_block(c_right, 3)
        yield
        sib_left_upper.wait_recv()
        sib_left_lower.wait_recv()
        on_block(c_left + 1 - 2 * k, 4)
        sib_right_lower.wait_recv()
        sib_right_upper.wait_recv()
        on_block(c_right + 1 - 2 * k, 5)
        onward_right.wait_recv()
        sib_opp_upper = copy_to(c_opp, upper, c_sib)
        onward_left.wait_recv()
        sib_opp_lower = copy_to(c_opp, lower, c_sib)
        on_block(c_opp, 6)
        sib_opp_upper.wait_recv()
        sib_opp_lower.wait_recv()
        on_block(c_opp + 1 - 2 * k, 7)

    def scatter(compute, h, part, sib, fwd, from_left, from_right, got):
        rows, upper, lower = half_rows(h)

        def pair(chip, slot):
            mine, theirs = chip * CORES + k, chip * CORES + 1 - k
            part[theirs, rows] = compute(theirs)
            copy = net.send(part.at[theirs, rows], sib.at[slot, rows], cols=c_sib)
            part[mine, rows] = compute(mine)
            return copy

        sib_opp = pair(opposite, 0)
        sib_right = pair(right, 1)
        sib_opp.wait_recv()
        part[c_opp, rows] = part[c_opp, rows] + sib[0, rows]
        fwd_upper = net.send(part.at[c_opp, upper], fwd.at[upper], cols=c_right)
        fwd_lower = net.send(part.at[c_opp, lower], fwd.at[lower], cols=c_left)
        sib_left = pair(left, 2)
        sib_right.wait_recv()
        part[c_right, rows] = part[c_right, rows] + sib[1, rows]
        right_lower = net.send(part.at[c_right, lower], from_left.at[lower], cols=c_right)
        sib_own = pair(x, 3)
        sib_left.wait_recv()
        part[c_left, rows] = part[c_left, rows] + sib[2, rows]
        left_upper = net.send(part.at[c_left, upper], from_right.at[upper], cols=c_left)
        yield
        fwd_upper.wait_recv()
        part[c_right, upper] = part[c_right, upper] + fwd[upper]
        right_upper = net.send(part.at[c_right, upper], from_left.at[upper], cols=c_right)
        fwd_lower.wait_recv()
        part[c_left, lower] = part[c_left, lower] + fwd[lower]
        left_lower = net.send(part.at[c_left, lower], from_right.at[lower], cols=c_left)
        yield
        sib_own.wait_recv()
        total = part[c, rows] + sib[3, rows]
        for copy in (right_lower, left_upper, right_upper, left_lower):
            copy.wait_recv()
        got.append(total + from_left[rows] + from_right[rows])

    share = half // ny

    def p_parts(at):
        lanes = pl.ds(pl.multiple_of(at * block, block), block)
        return p_high[:, lanes], p_low[:, lanes]

    def reduced_and_applied(value, at, h):
        own, yi, zi, to, ti, ia = (b.at[at, h] for b in (az, y_in, z_in, t_out, t_in, i_all))
        za, xa = z_all.at[at], x_all.at[at]
        y_rows = pl.ds(pl.multiple_of(h * half + y * share, share), share)
        own[...] = value
        copies = []
        for d in range(1, ny):
            rows = pl.ds(pl.multiple_of(lax.rem(y + d, ny) * share, share), share)
            copies.append(net.send(own.at[rows], yi.at[d - 1], rows=y_peer(d)))
        yield
        total = own[pl.ds(pl.multiple_of(y * share, share), share)]
        for d in range(1, ny):
            copies[d - 1].wait_recv()
            total = total + yi[d - 1]
        zi[z] = total
        copies = [net.send(zi.at[z], zi.at[z], rows=z_peer(d)) for d in range(1, nz)]
        yield
        for copy in copies:
            copy.wait_recv()
        total = zi[0]
        for i in range(1, nz):
            total = total + zi[i]
        za[y_rows] = total
        copies = []
        for d in range(1, PEERS):
            to[c_peer(d)] = with_parts(total, p_parts(c_peer(d)), NN)
            copies.append(net.send(to.at[c_peer(d)], ti.at[d - 1], cols=c_peer(d)))
        late = [net.send(za.at[y_rows], za.at[y_rows], rows=y_peer(d)) for d in range(1, ny)]
        total = with_parts(total, p_parts(c), NN)
        yield
        for d in range(1, PEERS):
            copies[d - 1].wait_recv()
            total = total + ti[d - 1]
        ia[c] = total
        copies = [net.send(ia.at[c], ia.at[c], cols=c_peer(d)) for d in range(1, PEERS)]
        total = with_parts(total, p_parts(c), NT)
        yield
        for d in range(1, PEERS):
            copies[d - 1].wait_recv()
            source = lax.rem(c + PEERS - d, PEERS)
            total = total + with_parts(ia[source], p_parts(source), NT)
        xa[y_rows] = total
        late += [net.send(xa.at[y_rows], xa.at[y_rows], rows=y_peer(d)) for d in range(1, ny)]
        yield
        for copy in late:
            copy.wait_recv()

    def row_sum(twice, at):
        buffer = c_in.at[at]
        buffer[c] = packed(twice)
        copies = [net.send(buffer.at[c], buffer.at[c], cols=c_peer(d)) for d in range(1, PEERS)]

        def end():
            for copy in copies:
                copy.wait_recv()
            total = buffer[0]
            for i in range(1, PEERS):
                total = total + buffer[i]
            return unpacked(total)

        return end

    def small_sum(value, at):
        piece = width // PEERS
        own, xb, zb, yb, out = (b.at[at] for b in (sm_own, sm_x, sm_z, sm_y, sm_out))
        own[...] = value
        copies = []
        for d in range(1, PEERS):
            rows = pl.ds(pl.multiple_of(c_peer(d) * piece, piece), piece)
            copies.append(net.send(own.at[rows], xb.at[d - 1], cols=c_peer(d)))
        yield
        mine = pl.ds(pl.multiple_of(c * piece, piece), piece)
        total = own[mine]
        for d in range(1, PEERS):
            copies[d - 1].wait_recv()
            total = total + xb[d - 1]
        zb[z] = total
        copies = [net.send(zb.at[z], zb.at[z], rows=z_peer(d)) for d in range(1, nz)]
        yield
        for copy in copies:
            copy.wait_recv()
        total = zb[0]
        for i in range(1, nz):
            total = total + zb[i]
        yb[y] = total
        copies = [net.send(yb.at[y], yb.at[y], rows=y_peer(d)) for d in range(1, ny)]
        yield
        for copy in copies:
            copy.wait_recv()
        total = yb[0]
        for i in range(1, ny):
            total = total + yb[i]
        out[mine] = total
        copies = [net.send(out.at[mine], out.at[mine], cols=c_peer(d)) for d in range(1, PEERS)]
        yield
        for copy in copies:
            copy.wait_recv()

    def through(full, at, before, after_right):
        sums = ([], [])

        def block_of(h):
            rows, _, _ = half_rows(h)

            def on_block(at, step):
                before(at, step, h)
                value = full[at, rows]
                term = with_counts(value, counts[chunk(at)], NN) * spread[at]
                term = term + jnp.sum(value, axis=1, keepdims=True) * lowest[at]
                sums[h].append(term if not sums[h] else sums[h][-1] + term)

            return on_block

        one, two = gather(full, 0, block_of(0)), gather(full, 1, block_of(1))
        next(one)
        next(one)
        next(two)
        next(one)
        next(two)
        finish(one)
        sum_one = reduced_and_applied(sums[0][-1], at, 0)
        next(sum_one)
        finish(two)
        next(sum_one)
        sum_two = reduced_and_applied(sums[1][-1], at, 1)
        next(sum_two)
        fill(4)
        next(sum_two)
        fill(4)
        next(sum_one)
        fill(2)
        next(sum_two)
        fill(4)
        next(sum_one)
        fill(2)
        next(sum_two)
        fill(4)
        next(sum_one)
        fill(2)
        next(sum_two)
        finish(sum_one)

        def forward(h, got):
            value = x_all[at, half_rows(h)[0]]

            def compute(j):
                at_lowest = jnp.sum(value * lowest[j], axis=1, keepdims=True)
                return with_counts(value * spread[j], counts[chunk(j)], NT) + at_lowest

            return scatter(compute, h, *(b.at[at] for b in (y_part, y_sib, y_fwd, y_left, y_right)), got)

        got = []
        one = forward(0, got)
        next(one)
        finish(sum_two)
        finish(work[0])
        work[0] = after_right()
        next(work[0])
        two = forward(1, got)
        next(two)
        next(one)
        fill(2)
        next(two)
        finish(work[0])
        finish(one)
        finish(two)
        return jnp.concatenate(got, axis=0)

    got = {}
    sums = small_sum(b_gram, 0)
    next(sums)

    def load(at, step, h):
        if h == 0:
            loads[step].wait()
            g = g_f32[chunk(at)]
            low = jnp.min(g, axis=0, keepdims=True)
            width_of = jnp.max(g, axis=0, keepdims=True) - low
            one, two = low + 0.25 * width_of, low + 0.75 * width_of
            counts[chunk(at)] = jnp.where(g > two, 2.0, jnp.where(g > one, 1.0, 0.0)).astype(BF16)
            lowest[at] = low
            spread[at] = 0.5 * width_of
        if (h, step) in ((0, 2), (0, 7), (1, 5)):
            next(sums)

    def orthonormal_first():
        finish(sums)
        yield
        done = []
        yield from eliminate([with_identity(sm_out[0])], [False], done)
        got["l0_inv"], got["l0_t"] = factors(done[0])
        yield
        u_one[...] = exact(got["l0_inv"], b_own[...])

    def orthonormal_right():
        l0_inv = got["l0_inv"]
        z_one, x_one = exact(l0_inv, z_all[0]), exact(l0_inv, x_all[0])
        end = row_sum(exact(z_one, doubled(x_one), NT), 0)
        yield
        done = []
        yield from eliminate([with_identity(end())], [False], done)
        got["l1_inv"], got["l1_t"] = factors(done[0])
        yield
        got["x_v"], got["z_v"] = exact(got["l1_inv"], x_one), exact(got["l1_inv"], z_one)
        got["back"] = exact(got["l1_t"], u_one[...])
        got["l1_l0"] = exact(got["l1_inv"], l0_inv)

    work[0] = orthonormal_first()
    y_one = through(b_full, 0, load, orthonormal_right)
    y_v = exact(got["l1_l0"], y_one)
    mapped = y_v - got["back"]
    n_full[c] = mapped
    x_v, z_v, l1_t = got["x_v"], got["z_v"], got["l1_t"]

    def first_target():
        row, lane = iotas(width, width)
        unit = jnp.where(row == lane, 1.0, 0.0)
        got["target_t"] = exact(unit, exact(l1_t, got["l0_t"]), NT)
        yield

    def second_factors():
        z_w, x_w = z_all[1], x_all[1]
        end_h_one = row_sum(exact(x_w, doubled(z_v), NT), 1)
        yield
        h_one = end_h_one()
        h = h_one[:, :width]
        z_j, x_j = z_w - exact(h, z_v), x_w - exact(h, x_v)
        end_e = row_sum(exact(z_j, doubled(x_j), NT), 2)
        normal = exact(l1_t, doubled(l1_t), NT) + h_one
        yield
        done = []
        yield from eliminate([with_identity(h_one), with_identity(normal)], [False, True], done)
        l2_inv, l2_t = factors(done[0])
        s_inv = done[1][:, :width]
        yield
        left_c = exact(l2_inv, end_e()[:, :width])
        c_two = exact(left_c, doubled(l2_inv), NT)
        c_half = c_two[:, :width]
        got["l2_inv"] = l2_inv
        got["back"] = exact(l2_t, y_v) + exact(exact(c_half, l2_inv), mapped)
        cross = exact(c_half, l2_t)
        x_ref[0] = x_v
        x_ref[1] = exact(l2_inv, x_j)
        m_ref[1] = exact(c_half, c_two) - exact(exact(cross, s_inv), doubled(cross), NT)
        m_ref[2] = exact(exact(got["target_t"], s_inv), doubled(cross), NT)
        m_ref[3] = exact(c_half, doubled_lanes(l2_t))
        m_ref[4] = done[1]
        m_ref[5] = doubled_lanes(got["target_t"])

    def doubled_lanes(value):
        row, lane = iotas(width, 2 * width)
        both = jnp.where(jnp.logical_or(lane == row, lane == row + width), 1.0, 0.0)
        return exact(value, both)

    work[0] = first_target()
    y_two = through(n_full, 1, lambda *_: None, second_factors)
    n_two = exact(got["l2_inv"], y_two) - got["back"]
    n_ref[...] = n_two
    finish(small_sum(exact(n_two, doubled(n_two), NT), 1))
    m_ref[0] = sm_out[1]
    net.finish()


def last_block(n_ref, x_ref, m_ref, s_ref, u_ref):
    width = n_ref.shape[0]
    h_two = m_ref[0]
    done = []
    systems = [with_identity(h_two), with_identity(h_two + m_ref[1])]
    for _ in eliminate(systems, [False, True], done):
        pass
    l3_inv, _ = factors(done[0])
    u_ref[...] = exact(l3_inv, n_ref[...])
    b_t = -exact(m_ref[2][:, :width], done[1][:, :width])
    a_t = exact(m_ref[5][:, :width] - exact(b_t, m_ref[3][:, :width]), m_ref[4][:, :width])
    s_ref[...] = SCALE * (exact(a_t, x_ref[0]) + exact(b_t, x_ref[1]))


def solution(mesh, ny=4):
    nrows = mesh.shape["rows"]
    nz = nrows // ny

    def per_device(genotypes, right_sides, inverse_r):
        rows, block = genotypes.shape
        rows_w, width = right_sides.shape
        variants = inverse_r.shape[1]
        half = width // 2
        share = half // ny
        piece = width // PEERS
        v = pltpu.VMEM
        any_space = pl.BlockSpec(memory_space=pl.ANY)
        vmem = pl.BlockSpec(memory_space=pltpu.VMEM)
        messages = 4 * (13 + 10) + 4 * (3 * (ny - 1) + nz - 1 + 2 * (PEERS - 1)) + 3 * (PEERS - 1)
        messages += 2 * (2 * (PEERS - 1) + nz + ny - 2)
        small = pl.pallas_call(
            functools.partial(body, nz, ny),
            out_shape=(
                jax.ShapeDtypeStruct((width, rows_w), F32),
                jax.ShapeDtypeStruct((2, width, block), F32),
                jax.ShapeDtypeStruct((6, width, 2 * width), F32),
            ),
            in_specs=[any_space] * 3,
            out_specs=[vmem] * 3,
            scratch_shapes=[
                v((rows, block), F32), v((width, rows_w), F32), v((block, variants), F32), v((rows, block), BF16),
                v((PEERS, 1, block), F32), v((PEERS, 1, block), F32),
                v((block, variants), BF16), v((block, variants), BF16),
                v((PEERS, width, rows_w), F32), v((PEERS, width, rows_w), F32), v((width, rows_w), F32),
                v((2, PEERS, width, rows_w), F32), v((2, CHIPS, width, rows_w), F32),
                v((2, width, rows_w), F32), v((2, width, rows_w), F32), v((2, width, rows_w), F32),
                v((2, 2, half, block), F32), v((2, 2, max(ny - 1, 1), share, block), F32), v((2, 2, nz, share, block), F32),
                v((2, 2, PEERS, share, block), F32), v((2, 2, PEERS - 1, share, block), F32),
                v((2, 2, PEERS, share, block), F32), v((2, width, block), F32), v((2, width, block), F32),
                v((3, PEERS, half, 2 * width), F32),
                v((2, width, 2 * width), F32), v((2, PEERS - 1, piece, 2 * width), F32),
                v((2, nz, piece, 2 * width), F32), v((2, ny, piece, 2 * width), F32),
                v((2, width, 2 * width), F32),
                pltpu.SemaphoreType.DMA((PEERS + 2,)),
                pltpu.SemaphoreType.DMA((messages,)),
                pltpu.SemaphoreType.DMA((messages,)),
            ],
            compiler_params=pltpu.CompilerParams(
                collective_id=0, has_side_effects=True, vmem_limit_bytes=58 * 1024 * 1024
            ),
        )(genotypes, right_sides.T, inverse_r)
        s_t, u_t = pl.pallas_call(
            last_block,
            out_shape=(
                jax.ShapeDtypeStruct((width, block), F32),
                jax.ShapeDtypeStruct((width, rows_w), F32),
            ),
        )(*small)
        return s_t.T, u_t.T

    in_specs = (P("rows", "cols"), P(("rows", "cols"), None), P("cols", None))
    out_specs = (P("cols", None), P(("rows", "cols"), None))
    return jax.shard_map(
        per_device, mesh=mesh, in_specs=in_specs, out_specs=out_specs, check_vma=False
    )
```

time: 182 us -> 148 us (0.81)
  Pallas kernels: 176 us -> 147 us
  local copies, waits for them, and re-layouts: 3.17 us -> 0 us
    pallas_call x1, Pallas kernels: 176 us -> 140 us  [per_device(): pl.pallas_call(functools.partial(body, nz, ny), out_shape=(jax.ShapeDtype...]
    pallas_call x0 -> x1, Pallas kernels: none -> 7.04 us  [per_device(): pl.pallas_call(last_block, out_shape=(jax.ShapeDtypeStruct((width, block)...]
    unnamed x2 -> x0, local copies, waits for them, and re-layouts: 3.17 us -> none
where the time goes in v2:
time: 148 us
  Pallas kernels  147 us (99%)
    pallas_call x1, Pallas kernels, per_device(): pl.pallas_call(functools.partial(body, nz, ny), out_shape=(jax.ShapeDtype...  140 us
    pallas_call x1, Pallas kernels, per_device(): pl.pallas_call(last_block, out_shape=(jax.ShapeDtypeStruct((width, block)...  7.04 us

profile of v2, /device:TPU:1, one launch (start us, length us, event | category | flops | bytes accessed | tf_op | source)
XLA Modules:
  0.0 148.1 jit_solution(1569127145778555634)
XLA Ops:
  0.6 140.4 %shard_map.50 = (f32[64,1152]{1,0:T(8,128)}, f32[2,64,256]{2,1,0:T(8,128)}, f32[6,64,128]{2,1,0:T(8,128)}) custom-call(f32[9216,256]{1,0:T(8,128)} %g_hbm.1, f32[64,1152]{1,0:T(8,128)} %bitcast.3, f32[256,2048]{1,0:T(8,128)} %p_hbm.1), custom_call_target="tpu_custom_call" | custom-call | tf_op jit(solution)/shard_map/pallas_call | solution.py:614
  141.1 7.0 %shard_map.51 = (f32[64,256]{1,0:T(8,128)}, f32[64,1152]{1,0:T(8,128)}) custom-call(f32[64,1152]{1,0:T(8,128)} %get-tuple-element.7.n_ref, f32[2,64,256]{2,1,0:T(8,128)} %get-tuple-element.8.x_ref, f32[6,64,128]{2,1,0:T(8,128)} %get-tuple-element.9.m_ref), custom_call_target="tpu_custom_call" | custom-call | tf_op jit(solution)/shard_map/pallas_call | solution.py:645

commit v3 on v2

v3 whole, which is shorter than its diff:
```python
import functools

import jax
import jax.numpy as jnp
from jax import lax
from jax.experimental import pallas as pl
from jax.experimental.pallas import tpu as pltpu
from jax.sharding import PartitionSpec as P

F32 = jnp.float32
BF16 = jnp.bfloat16
NN = (((1,), (0,)), ((), ()))
NT = (((1,), (1,)), ((), ()))
CHIPS = 4
CORES = 2
PEERS = CHIPS * CORES
SCALE = 4096.0


def exact(left, right, dims=NN):
    return lax.dot_general(
        left, right, dims, precision=lax.Precision.HIGHEST, preferred_element_type=F32
    )


def dot(left, right, dims):
    return lax.dot_general(left, right, dims, preferred_element_type=F32)


def parts(value):
    high = value.astype(BF16).astype(F32)
    rest = value - high
    middle = rest.astype(BF16).astype(F32)
    return high, middle, rest - middle


def stacked_parts(value):
    rows = value.shape[0]
    stack = jnp.concatenate(parts(value), axis=0)
    if 3 * rows % 16:
        stack = jnp.concatenate([stack, jnp.zeros((16 - 3 * rows % 16, value.shape[1]), F32)], axis=0)
    return stack.astype(BF16)


def with_counts(value, counts, dims):
    rows = value.shape[0]
    out = dot(stacked_parts(value), counts, dims)
    return out[2 * rows : 3 * rows] + out[rows : 2 * rows] + out[:rows]


def with_parts(value, right, dims):
    rows = value.shape[0]
    stack = stacked_parts(value)
    first = dot(stack, right[0], dims)
    second = dot(stack[: max(2 * rows, 16)], right[1], dims)
    small = first[2 * rows : 3 * rows] + second[rows : 2 * rows]
    return small + (first[rows : 2 * rows] + second[:rows]) + first[:rows]


def beside(value):
    size, lanes = value.shape
    _, lane = iotas(size, lanes)
    return jnp.where(lane < size, value, pltpu.roll(value, size, 1))


def side_by_side(one, two):
    size, lanes = one.shape
    return jnp.where(iotas(size, lanes)[1] < size, one, two)


def doubled(rows):
    return jnp.concatenate([rows, rows], axis=0)


def iotas(rows, lanes):
    row = lax.broadcasted_iota(jnp.int32, (rows, lanes), 0)
    lane = lax.broadcasted_iota(jnp.int32, (rows, lanes), 1)
    return row, lane


def with_identity(twice):
    size = twice.shape[0]
    row, lane = iotas(size, 2 * size)
    return jnp.where(lane < size, jnp.where(lane == row, 1.0, 0.0), twice)


def eliminate(systems, full, done, stride=4):
    size = systems[0].shape[0]
    shape = (size, 2 * size)
    row_at, _ = iotas(*shape)
    systems = list(systems)
    for j in range(0, size, 2):
        for i, m in enumerate(systems):
            first = jnp.broadcast_to(m[:, size + j : size + j + 1], shape)
            second = jnp.broadcast_to(m[:, size + j + 1 : size + j + 2], shape)
            top, bottom = m[j : j + 1, :], m[j + 1 : j + 2, :]
            inverse = 1.0 / first[j : j + 1, :]
            ratio = first[j + 1 : j + 2, :] * inverse
            across = second[j : j + 1, :]
            pivot = 1.0 / (second[j + 1 : j + 2, :] - ratio * across)
            row_two = (bottom - ratio * top) * pivot
            row_one = (top - across * row_two) * inverse
            less = m - first * row_one - second * row_two
            if full[i]:
                systems[i] = jnp.where(row_at == j, row_one, jnp.where(row_at == j + 1, row_two, less))
            else:
                systems[i] = jnp.where(row_at > j + 1, less, m)
        if j // 2 % stride == stride - 1:
            yield
    done.extend(systems)


def factors(m):
    size = m.shape[0]
    row, lane = iotas(size, 2 * size)
    odd = lax.rem(row, 2) == 1
    above = pltpu.roll(m, 1, 0)
    left = jnp.logical_and(odd, lane == row + size - 1)
    under = jnp.sum(jnp.where(left, m, 0.0), axis=1, keepdims=True)
    over = jnp.sum(jnp.where(left, above, jnp.where(jnp.logical_and(lane == 0, jnp.logical_not(odd)), 1.0, 0.0)), axis=1, keepdims=True)
    m = m - (under / over) * above
    pivots = jnp.sum(jnp.where(lane == row + size, m, 0.0), axis=1, keepdims=True)
    scaled = lax.rsqrt(pivots) * m
    upper = pltpu.roll(jnp.where(lane >= row + size, scaled, 0.0), size, 1)
    return beside(scaled), beside(upper)


def packed(twice):
    half = twice.shape[0] // 2
    _, lane = iotas(half, twice.shape[1])
    return jnp.where(lane < twice.shape[1] // 2, twice[:half], twice[half:])


def unpacked(pack):
    half, lanes = pack.shape
    _, lane = iotas(half, lanes)
    other = pltpu.roll(pack, lanes // 2, 1)
    first = lane < lanes // 2
    return jnp.concatenate([jnp.where(first, pack, other), jnp.where(first, other, pack)], axis=0)


class Net:
    def __init__(self, send_sems, recv_sems):
        self.send_sems, self.recv_sems = send_sems, recv_sems
        self.groups, self.arrivals = 0, 0
        self.sent = []

    def group(self, like, together=True):
        sem = self.send_sems.at[self.groups]
        self.groups += 1
        self.sent.append((like, sem))
        arrival = self.next_arrival() if together else None

        def send(source, target, **device):
            copy = pltpu.make_async_remote_copy(
                src_ref=source,
                dst_ref=target,
                send_sem=sem,
                recv_sem=arrival if together else self.next_arrival(),
                device_id=device,
                device_id_type=pl.DeviceIdType.MESH,
            )
            copy.start()
            return copy

        def arrive():
            pltpu.make_async_copy(like, like, arrival).wait()

        return send, arrive

    def next_arrival(self):
        self.arrivals += 1
        return self.recv_sems.at[self.arrivals - 1]

    def finish(self):
        for like, sem in self.sent:
            pltpu.make_async_copy(like, like, sem).wait()


def body(
    nz, ny,
    g_hbm, b_hbm, p_hbm, n_ref, x_ref, m_ref,
    g_f32, b_own, p_f32, counts, lowest, spread, p_high, p_low,
    b_full, n_full, u_one, back,
    y_part, y_sib, y_fwd, y_left, y_right,
    az, z_in, y_in, t_out, t_in, i_all, z_all, x_all,
    c_in, sm_own, sm_x, sm_z, sm_y, sm_out,
    g_sems, send_sems, recv_sems,
):
    width, rows_w = b_own.shape
    block = p_f32.shape[0]
    half = width // 2
    r, c = lax.axis_index("rows"), lax.axis_index("cols")
    x, k = c // CORES, c % CORES
    z, y = r // ny, r % ny
    right = lax.rem(x + 1, CHIPS)
    left = lax.rem(x + CHIPS - 1, CHIPS)
    opposite = lax.rem(x + 2, CHIPS)
    c_sib = x * CORES + 1 - k
    c_right, c_left, c_opp = (chip * CORES + k for chip in (right, left, opposite))
    net = Net(send_sems, recv_sems)

    def chunk(at):
        return pl.ds(pl.multiple_of(at * rows_w, rows_w), rows_w)

    def c_peer(d):
        return lax.rem(c + d, PEERS)

    def z_peer(d):
        return lax.rem(z + d, nz) * ny + y

    def y_peer(d):
        return z * ny + lax.rem(y + d, ny)

    barrier = pltpu.get_barrier_semaphore()
    greeted = [{"rows": z_peer(d)} for d in range(1, nz)]
    greeted += [{"rows": y_peer(d)} for d in range(1, ny)]
    greeted += [{"cols": c_peer(d)} for d in range(1, PEERS)]
    for device in greeted:
        pl.semaphore_signal(barrier, inc=1, device_id=device, device_id_type=pl.DeviceIdType.MESH)

    own_load = pltpu.make_async_copy(b_hbm, b_own, g_sems.at[PEERS])
    p_load = pltpu.make_async_copy(p_hbm, p_f32, g_sems.at[PEERS + 1])
    own_load.start()
    loads = []
    for step, at in enumerate((c, c_sib, c_left, c_right, c_left + 1 - 2 * k, c_right + 1 - 2 * k, c_opp, c_opp + 1 - 2 * k)):
        copy = pltpu.make_async_copy(g_hbm.at[chunk(at)], g_f32.at[chunk(at)], g_sems.at[step])
        copy.start()
        loads.append(copy)
    p_load.start()
    own_load.wait()
    b_own[...] = b_own[...] * (1.0 / SCALE)
    b_full[c] = b_own[...]
    b_gram = exact(b_own[...], doubled(b_own[...]), NT)
    p_load.wait()
    p_high[...], p_low[...] = (v.astype(BF16) for v in parts(p_f32[...])[:2])
    pl.semaphore_wait(barrier, len(greeted))

    work = [iter(())]
    got = {}

    def fill(pieces):
        for _ in range(pieces):
            next(work[0], None)

    def finish(steps):
        for _ in steps:
            pass

    upper, lower = pl.ds(0, half), pl.ds(half, half)
    tiles = rows_w // 128
    cut = (tiles + 1) // 2 * 128
    pieces = (pl.ds(0, cut), pl.ds(cut, rows_w - cut)) if tiles > 1 else (pl.ds(0, rows_w),)
    whole = pl.ds(0, rows_w)

    def samples(at, lanes):
        return pl.ds(pl.multiple_of(at * rows_w + lanes.start, 128), lanes.size)

    def gather(full, lanes, on_block):
        send, _ = net.group(full.at[pl.ds(0, PEERS - 1), :, lanes], together=False)

        def copy_to(at, rows, target):
            return send(full.at[at, rows, lanes], full.at[at, rows, lanes], cols=target)

        right_upper = copy_to(c, upper, c_right)
        left_lower = copy_to(c, lower, c_left)
        right_lower = copy_to(c, lower, c_right)
        left_upper = copy_to(c, upper, c_left)
        sib_own = send(full.at[c, :, lanes], full.at[c, :, lanes], cols=c_sib)
        yield
        on_block(c, 0)
        right_upper.wait_recv()
        onward_right = copy_to(c_left, upper, c_right)
        sib_left_upper = copy_to(c_left, upper, c_sib)
        left_lower.wait_recv()
        onward_left = copy_to(c_right, lower, c_left)
        sib_right_lower = copy_to(c_right, lower, c_sib)
        yield
        sib_own.wait_recv()
        on_block(c_sib, 1)
        right_lower.wait_recv()
        sib_left_lower = copy_to(c_left, lower, c_sib)
        left_upper.wait_recv()
        sib_right_upper = copy_to(c_right, upper, c_sib)
        on_block(c_left, 2)
        on_block(c_right, 3)
        sib_left_upper.wait_recv()
        sib_left_lower.wait_recv()
        on_block(c_left + 1 - 2 * k, 4)
        sib_right_lower.wait_recv()
        sib_right_upper.wait_recv()
        on_block(c_right + 1 - 2 * k, 5)
        onward_right.wait_recv()
        sib_opp_upper = copy_to(c_opp, upper, c_sib)
        onward_left.wait_recv()
        sib_opp_lower = copy_to(c_opp, lower, c_sib)
        on_block(c_opp, 6)
        sib_opp_upper.wait_recv()
        sib_opp_lower.wait_recv()
        on_block(c_opp + 1 - 2 * k, 7)

    def scatter(compute, lanes, part, sib, fwd, from_left, from_right, got):
        send, _ = net.group(part.at[pl.ds(0, PEERS - 1), :, lanes], together=False)

        def pair(chip, slot):
            mine, theirs = chip * CORES + k, chip * CORES + 1 - k
            part[theirs, :, lanes] = compute(theirs)
            copy = send(part.at[theirs, :, lanes], sib.at[slot, :, lanes], cols=c_sib)
            part[mine, :, lanes] = compute(mine)
            return copy

        sib_opp = pair(opposite, 0)
        sib_right = pair(right, 1)
        sib_opp.wait_recv()
        part[c_opp, :, lanes] = part[c_opp, :, lanes] + sib[0, :, lanes]
        fwd_upper = send(part.at[c_opp, upper, lanes], fwd.at[upper, lanes], cols=c_right)
        fwd_lower = send(part.at[c_opp, lower, lanes], fwd.at[lower, lanes], cols=c_left)
        yield
        sib_left = pair(left, 2)
        sib_right.wait_recv()
        part[c_right, :, lanes] = part[c_right, :, lanes] + sib[1, :, lanes]
        right_lower = send(part.at[c_right, lower, lanes], from_left.at[lower, lanes], cols=c_right)
        sib_own = pair(x, 3)
        sib_left.wait_recv()
        part[c_left, :, lanes] = part[c_left, :, lanes] + sib[2, :, lanes]
        left_upper = send(part.at[c_left, upper, lanes], from_right.at[upper, lanes], cols=c_left)
        yield
        fwd_upper.wait_recv()
        part[c_right, upper, lanes] = part[c_right, upper, lanes] + fwd[upper, lanes]
        right_upper = send(part.at[c_right, upper, lanes], from_left.at[upper, lanes], cols=c_right)
        fwd_lower.wait_recv()
        part[c_left, lower, lanes] = part[c_left, lower, lanes] + fwd[lower, lanes]
        left_lower = send(part.at[c_left, lower, lanes], from_right.at[lower, lanes], cols=c_left)
        yield
        sib_own.wait_recv()
        total = part[c, :, lanes] + sib[3, :, lanes]
        for copy in (right_lower, left_upper, right_upper, left_lower):
            copy.wait_recv()
        got.append(total + from_left[:, lanes] + from_right[:, lanes])

    share = width // nz
    z_rows = pl.ds(pl.multiple_of(z * share, share), share)

    def p_parts(at):
        lanes = pl.ds(pl.multiple_of(at * block, block), block)
        return p_high[:, lanes], p_low[:, lanes]

    def reduced_and_applied(value, at):
        lanes = pl.ds(0, value.shape[1])
        own, zi, yi, to, ti, ia, za, xa = (b.at[at] for b in (az, z_in, y_in, t_out, t_in, i_all, z_all, x_all))
        own[:, lanes] = value
        send, arrive = net.group(zi.at[:, :, lanes])
        for d in range(1, nz):
            rows = pl.ds(pl.multiple_of(lax.rem(z + d, nz) * share, share), share)
            send(own.at[rows, lanes], zi.at[d - 1, :, lanes], rows=z_peer(d))
        yield
        total = own[z_rows, lanes]
        arrive()
        for d in range(1, nz):
            total = total + zi[d - 1, :, lanes]
        yi[y, :, lanes] = total
        if ny > 1:
            send, arrive = net.group(yi.at[pl.ds(0, ny - 1), :, lanes])
            for d in range(1, ny):
                send(yi.at[y, :, lanes], yi.at[y, :, lanes], rows=y_peer(d))
        yield
        if ny > 1:
            arrive()
        total = yi[0, :, lanes]
        for i in range(1, ny):
            total = total + yi[i, :, lanes]
        za[z_rows, lanes] = total
        total = total[:, :block]
        send, arrive = net.group(ti)
        for d in range(1, PEERS):
            to[c_peer(d)] = with_parts(total, p_parts(c_peer(d)), NN)
            send(to.at[c_peer(d)], ti.at[d - 1], cols=c_peer(d))
        send, got["summed"] = net.group(za.at[pl.ds(0, (nz - 1) * share), lanes])
        for d in range(1, nz):
            send(za.at[z_rows, lanes], za.at[z_rows, lanes], rows=z_peer(d))
        total = with_parts(total, p_parts(c), NN)
        yield
        arrive()
        for d in range(1, PEERS):
            total = total + ti[d - 1]
        ia[c] = total
        send, arrive = net.group(ia.at[pl.ds(0, PEERS - 1)])
        for d in range(1, PEERS):
            send(ia.at[c], ia.at[c], cols=c_peer(d))
        total = with_parts(total, p_parts(c), NT)
        yield
        arrive()
        for d in range(1, PEERS):
            source = lax.rem(c + PEERS - d, PEERS)
            total = total + with_parts(ia[source], p_parts(source), NT)
        xa[z_rows] = total
        send, arrive = net.group(xa.at[pl.ds(0, (nz - 1) * share)])
        for d in range(1, nz):
            send(xa.at[z_rows], xa.at[z_rows], rows=z_peer(d))
        yield
        arrive()

    def row_sum(twice, at):
        buffer = c_in.at[at]
        buffer[c] = packed(twice)
        send, arrive = net.group(buffer.at[pl.ds(0, PEERS - 1)])
        for d in range(1, PEERS):
            send(buffer.at[c], buffer.at[c], cols=c_peer(d))

        def end():
            arrive()
            total = buffer[0]
            for i in range(1, PEERS):
                total = total + buffer[i]
            return unpacked(total)

        return end

    def small_sum(value):
        piece = width // PEERS
        mine = pl.ds(pl.multiple_of(c * piece, piece), piece)
        sm_own[...] = value
        send, arrive = net.group(sm_x)
        for d in range(1, PEERS):
            rows = pl.ds(pl.multiple_of(c_peer(d) * piece, piece), piece)
            send(sm_own.at[rows], sm_x.at[d - 1], cols=c_peer(d))
        yield
        total = sm_own[mine]
        arrive()
        for d in range(1, PEERS):
            total = total + sm_x[d - 1]
        sm_z[z] = total
        send, arrive = net.group(sm_z.at[pl.ds(0, nz - 1)])
        for d in range(1, nz):
            send(sm_z.at[z], sm_z.at[z], rows=z_peer(d))
        yield
        arrive()
        total = sm_z[0]
        for i in range(1, nz):
            total = total + sm_z[i]
        sm_y[y] = total
        if ny > 1:
            send, arrive = net.group(sm_y.at[pl.ds(0, ny - 1)])
            for d in range(1, ny):
                send(sm_y.at[y], sm_y.at[y], rows=y_peer(d))
        yield
        if ny > 1:
            arrive()
        total = sm_y[0]
        for i in range(1, ny):
            total = total + sm_y[i]
        sm_out[mine] = total
        send, arrive = net.group(sm_out.at[pl.ds(0, width - piece)])
        for d in range(1, PEERS):
            send(sm_out.at[mine], sm_out.at[mine], cols=c_peer(d))
        yield
        arrive()

    def backward(full, lanes, sums, before=lambda at, step: None):
        def on_block(at, step):
            before(at, step)
            value = full[at, :, lanes]
            term = with_counts(value, counts[samples(at, lanes)], NN) * spread[at]
            term = term + jnp.sum(value, axis=1, keepdims=True) * lowest[at]
            sums.append(term if not sums else sums[-1] + term)

        return gather(full, lanes, on_block)

    def forward(value, lanes, at, got):
        def compute(j):
            at_lowest = jnp.sum(value * lowest[j], axis=1, keepdims=True)
            return with_counts(value * spread[j], counts[samples(j, lanes)], NT) + at_lowest

        return scatter(compute, lanes, *(b.at[at] for b in (y_part, y_sib, y_fwd, y_left, y_right)), got)

    def in_shares(value, at):
        for step, _ in enumerate(reduced_and_applied(value, at)):
            if step >= 3:
                fill(6)
        finish(work[0])
        return z_all[at], x_all[at]

    end_gram = row_sum(b_gram, 0)

    def load(at, step):
        loads[step].wait()
        g = g_f32[chunk(at)]
        low = jnp.min(g, axis=0, keepdims=True)
        width_of = jnp.max(g, axis=0, keepdims=True) - low
        one, two = low + 0.25 * width_of, low + 0.75 * width_of
        counts[chunk(at)] = jnp.where(g > two, 2.0, jnp.where(g > one, 1.0, 0.0)).astype(BF16)
        lowest[at] = low
        spread[at] = 0.5 * width_of

    def orthonormal_first():
        got["summed"]()
        done = []
        yield from eliminate([with_identity(z_all[0, :, block:])], [False], done)
        got["two_l0_inv"], two_l0_t = factors(done[0])
        got["l0_inv"], got["l0_t"] = got["two_l0_inv"][:, :width], two_l0_t[:, :width]
        yield
        u_one[...] = exact(got["l0_inv"], b_own[...])

    totals = []
    finish(backward(b_full, whole, totals, load))
    work[0] = orthonormal_first()
    z_raw, x_raw = in_shares(jnp.concatenate([totals[-1], end_gram()], axis=1), 0)
    z_raw = z_raw[:, :block]

    def orthonormal_right():
        l0_inv = got["l0_inv"]
        z_one, x_one = exact(l0_inv, z_raw), exact(l0_inv, x_raw)
        end = row_sum(exact(z_one, doubled(x_one), NT), 1)
        yield
        done = []
        yield from eliminate([with_identity(end())], [False], done)
        two_l1_inv, got["two_l1_t"] = factors(done[0])
        got["l1_inv"], got["l1_t"] = two_l1_inv[:, :width], got["two_l1_t"][:, :width]
        got["left"] = side_by_side(exact(got["l1_inv"], got["two_l0_inv"]), -got["two_l1_t"])
        got["one"] = x_one, z_one

    work[0] = orthonormal_right()
    halves = []
    scatters = [forward(x_raw, lanes, 0, halves) for lanes in pieces]
    first, second = scatters[0], scatters[-1]
    fill(1)
    next(first)
    next(first)
    next(second)
    fill(3)
    next(first)
    next(second)
    fill(4)
    next(second)
    finish(work[0])
    l1_t = got["l1_t"]
    totals, gathers = [], []
    for lanes, steps in zip(pieces, scatters):
        finish(steps)
        n_full[c, :, lanes] = exact(got["left"], jnp.concatenate([halves[-1], u_one[:, lanes]], axis=0))
        gathers.append(backward(n_full, lanes, totals))
        next(gathers[-1])
    x_v, z_v = (exact(got["l1_inv"], v) for v in got["one"])
    for steps in gathers:
        next(steps)
    for steps in gathers:
        finish(steps)

    def first_target():
        got["summed"]()
        row, lane = iotas(width, width)
        unit = jnp.where(row == lane, 1.0, 0.0)
        got["target_t"] = exact(unit, exact(l1_t, got["l0_t"]), NT)
        yield

    def second_factors():
        end_h_one = row_sum(exact(x_w, doubled(z_v), NT), 2)
        yield
        h_one = end_h_one()
        h = h_one[:, :width]
        z_j, x_j = z_w - exact(h, z_v), x_w - exact(h, x_v)
        end_e = row_sum(exact(z_j, doubled(x_j), NT), 3)
        normal = exact(l1_t, doubled(l1_t), NT) + h_one
        yield
        done = []
        yield from eliminate([with_identity(h_one), with_identity(normal)], [False, True], done)
        two_l2_inv, two_l2_t = factors(done[0])
        l2_inv, l2_t = two_l2_inv[:, :width], two_l2_t[:, :width]
        s_inv = done[1][:, :width]
        yield
        left_c = exact(l2_inv, end_e()[:, :width])
        c_two = exact(left_c, doubled(l2_inv), NT)
        c_half = c_two[:, :width]
        got["l2_inv"] = l2_inv
        back_left = side_by_side(two_l2_t + exact(c_half, two_l2_inv), exact(l2_t, got["two_l1_t"]))
        back[...] = exact(back_left, jnp.concatenate([n_full[c], u_one[...]], axis=0))
        got["second"] = x_j, l2_inv, two_l2_t, s_inv, done[1], c_half, c_two

    def rest():
        x_j, l2_inv, two_l2_t, s_inv, s_full, c_half, c_two = got["second"]
        two_cross = exact(c_half, two_l2_t)
        cross = two_cross[:, :width]
        x_ref[0] = x_v
        x_ref[1] = exact(l2_inv, x_j)
        m_ref[1] = exact(c_half, c_two) - exact(exact(cross, s_inv), doubled(cross), NT)
        yield
        m_ref[2] = exact(exact(got["target_t"], s_inv), doubled(cross), NT)
        m_ref[3] = two_cross
        m_ref[4] = s_full
        m_ref[5] = doubled_lanes(got["target_t"])

    def doubled_lanes(value):
        row, lane = iotas(width, 2 * width)
        both = jnp.where(jnp.logical_or(lane == row, lane == row + width), 1.0, 0.0)
        return exact(value, both)

    work[0] = first_target()
    z_w, x_w = in_shares(totals[-1], 1)
    z_w = z_w[:, :block]
    work[0] = second_factors()
    halves = []
    scatters = [forward(x_w, lanes, 1, halves) for lanes in pieces]
    first, second = scatters[0], scatters[-1]
    fill(1)
    next(first)
    next(first)
    next(second)
    fill(2)
    next(first)
    next(second)
    fill(2)
    next(second)
    finish(work[0])
    n_gram = None
    for lanes, steps in zip(pieces, scatters):
        finish(steps)
        n_two = exact(got["l2_inv"], halves[-1]) - back[:, lanes]
        n_ref[:, lanes] = n_two
        term = exact(n_two, doubled(n_two), NT)
        n_gram = term if n_gram is None else n_gram + term
    work[0] = rest()
    for _ in small_sum(n_gram):
        fill(1)
    finish(work[0])
    m_ref[0] = sm_out[...]
    net.finish()


def last_block(n_ref, x_ref, m_ref, s_ref, u_ref):
    width = n_ref.shape[0]
    h_two = m_ref[0]
    done = []
    systems = [with_identity(h_two), with_identity(h_two + m_ref[1])]
    for _ in eliminate(systems, [False, True], done):
        pass
    l3_inv, _ = factors(done[0])
    u_ref[...] = exact(l3_inv[:, :width], n_ref[...])
    b_t = -exact(m_ref[2][:, :width], done[1][:, :width])
    a_t = exact(m_ref[5][:, :width] - exact(b_t, m_ref[3][:, :width]), m_ref[4][:, :width])
    s_ref[...] = SCALE * (exact(a_t, x_ref[0]) + exact(b_t, x_ref[1]))


def solution(mesh, ny=4):
    nrows = mesh.shape["rows"]
    nz = nrows // ny

    def per_device(genotypes, right_sides, inverse_r):
        rows, block = genotypes.shape
        rows_w, width = right_sides.shape
        variants = inverse_r.shape[1]
        half = width // 2
        share = width // nz
        piece = width // PEERS
        v = pltpu.VMEM
        any_space = pl.BlockSpec(memory_space=pl.ANY)
        vmem = pl.BlockSpec(memory_space=pltpu.VMEM)
        beside = block + 2 * width
        together = 2 * 6 + 4 + 4
        groups = together + 3 + 4
        arrivals = together + 3 * 13 + 4 * 10
        small = pl.pallas_call(
            functools.partial(body, nz, ny),
            out_shape=(
                jax.ShapeDtypeStruct((width, rows_w), F32),
                jax.ShapeDtypeStruct((2, width, block), F32),
                jax.ShapeDtypeStruct((6, width, 2 * width), F32),
            ),
            in_specs=[any_space] * 3,
            out_specs=[vmem] * 3,
            scratch_shapes=[
                v((rows, block), F32), v((width, rows_w), F32), v((block, variants), F32), v((rows, block), BF16),
                v((PEERS, 1, block), F32), v((PEERS, 1, block), F32),
                v((block, variants), BF16), v((block, variants), BF16),
                v((PEERS, width, rows_w), F32), v((PEERS, width, rows_w), F32),
                v((width, rows_w), F32), v((width, rows_w), F32),
                v((2, PEERS, width, rows_w), F32), v((2, CHIPS, width, rows_w), F32),
                v((2, width, rows_w), F32), v((2, width, rows_w), F32), v((2, width, rows_w), F32),
                v((2, width, beside), F32), v((2, nz - 1, share, beside), F32), v((2, ny, share, beside), F32),
                v((2, PEERS, share, block), F32), v((2, PEERS - 1, share, block), F32),
                v((2, PEERS, share, block), F32), v((2, width, beside), F32), v((2, width, block), F32),
                v((4, PEERS, half, 2 * width), F32),
                v((width, 2 * width), F32), v((PEERS - 1, piece, 2 * width), F32),
                v((nz, piece, 2 * width), F32), v((ny, piece, 2 * width), F32), v((width, 2 * width), F32),
                pltpu.SemaphoreType.DMA((PEERS + 2,)),
                pltpu.SemaphoreType.DMA((groups,)),
                pltpu.SemaphoreType.DMA((arrivals,)),
            ],
            compiler_params=pltpu.CompilerParams(
                collective_id=0, has_side_effects=True, vmem_limit_bytes=58 * 1024 * 1024
            ),
        )(genotypes, right_sides.T, inverse_r)
        s_t, u_t = pl.pallas_call(
            last_block,
            out_shape=(
                jax.ShapeDtypeStruct((width, block), F32),
                jax.ShapeDtypeStruct((width, rows_w), F32),
            ),
        )(*small)
        return s_t.T, u_t.T

    in_specs = (P("rows", "cols"), P(("rows", "cols"), None), P("cols", None))
    out_specs = (P("cols", None), P(("rows", "cols"), None))
    return jax.shard_map(
        per_device, mesh=mesh, in_specs=in_specs, out_specs=out_specs, check_vma=False
    )
```

time: 148 us -> 143 us (0.966)
  Pallas kernels: 147 us -> 143 us
    pallas_call x1, Pallas kernels: 140 us -> 136 us  [per_device(): pl.pallas_call(functools.partial(body, nz, ny), out_shape=(jax.ShapeDtype...]
where the time goes in v3:
time: 143 us
  Pallas kernels  143 us (100%)
    pallas_call x1, Pallas kernels, per_device(): pl.pallas_call(functools.partial(body, nz, ny), out_shape=(jax.ShapeDtype...  136 us
    pallas_call x1, Pallas kernels, per_device(): pl.pallas_call(last_block, out_shape=(jax.ShapeDtypeStruct((width, block)...  6.87 us

profile of v3, /device:TPU:1, one launch (start us, length us, event | category | flops | bytes accessed | tf_op | source)
XLA Modules:
  0.0 143.2 jit_solution(17985748192476833620)
XLA Ops:
  0.6 135.7 %shard_map.50 = (f32[64,1152]{1,0:T(8,128)}, f32[2,64,256]{2,1,0:T(8,128)}, f32[6,64,128]{2,1,0:T(8,128)}) custom-call(f32[9216,256]{1,0:T(8,128)} %g_hbm.1, f32[64,1152]{1,0:T(8,128)} %bitcast.3, f32[256,2048]{1,0:T(8,128)} %p_hbm.1), custom_call_target="tpu_custom_call" | custom-call | tf_op jit(solution)/shard_map/pallas_call | solution.py:661
  136.3 6.9 %shard_map.51 = (f32[64,256]{1,0:T(8,128)}, f32[64,1152]{1,0:T(8,128)}) custom-call(f32[64,1152]{1,0:T(8,128)} %get-tuple-element.7.n_ref, f32[2,64,256]{2,1,0:T(8,128)} %get-tuple-element.8.x_ref, f32[6,64,128]{2,1,0:T(8,128)} %get-tuple-element.9.m_ref), custom_call_target="tpu_custom_call" | custom-call | tf_op jit(solution)/shard_map/pallas_call | solution.py:692

commit v4 on v3

--- a/solution.py
+++ b/solution.py
@@ -223,7 +223,8 @@
     p_load = pltpu.make_async_copy(p_hbm, p_f32, g_sems.at[PEERS + 1])
     own_load.start()
     loads = []
-    for step, at in enumerate((c, c_sib, c_left, c_right, c_left + 1 - 2 * k, c_right + 1 - 2 * k, c_opp, c_opp + 1 - 2 * k)):
+    order = (c, c_sib, c_left, c_right, c_left + 1 - 2 * k, c_right + 1 - 2 * k, c_opp, c_opp + 1 - 2 * k)
+    for step, at in enumerate(order):
         copy = pltpu.make_async_copy(g_hbm.at[chunk(at)], g_f32.at[chunk(at)], g_sems.at[step])
         copy.start()
         loads.append(copy)
@@ -475,14 +476,15 @@
 
     def in_shares(value, at):
         for step, _ in enumerate(reduced_and_applied(value, at)):
-            if step >= 3:
-                fill(6)
+            if step >= 4:
+                fill(12)
         finish(work[0])
         return z_all[at], x_all[at]
 
     end_gram = row_sum(b_gram, 0)
 
-    def load(at, step):
+    def load(step):
+        at = order[step]
         loads[step].wait()
         g = g_f32[chunk(at)]
         low = jnp.min(g, axis=0, keepdims=True)
@@ -492,6 +494,10 @@
         lowest[at] = low
         spread[at] = 0.5 * width_of
 
+    def load_ahead(at, step):
+        for later in ((0, 1, 2, 3), (4, 5), (6,), (7,))[step] if step < 4 else ():
+            load(later)
+
     def orthonormal_first():
         got["summed"]()
         done = []
@@ -502,7 +508,7 @@
         u_one[...] = exact(got["l0_inv"], b_own[...])
 
     totals = []
-    finish(backward(b_full, whole, totals, load))
+    finish(backward(b_full, whole, totals, load_ahead))
     work[0] = orthonormal_first()
     z_raw, x_raw = in_shares(jnp.concatenate([totals[-1], end_gram()], axis=1), 0)
     z_raw = z_raw[:, :block]

time: 143 us -> 142 us (level)
  Pallas kernels: 143 us -> 141 us
where the time goes in v4:
time: 142 us
  Pallas kernels  141 us (99%)
    pallas_call x1, Pallas kernels, per_device(): pl.pallas_call(functools.partial(body, nz, ny), out_shape=(jax.ShapeDtype...  134 us
    pallas_call x1, Pallas kernels, per_device(): pl.pallas_call(last_block, out_shape=(jax.ShapeDtypeStruct((width, block)...  6.86 us

profile of v4, /device:TPU:1, one launch (start us, length us, event | category | flops | bytes accessed | tf_op | source)
XLA Modules:
  0.0 141.9 jit_solution(5379103966806700195)
XLA Ops:
  0.6 134.4 %shard_map.50 = (f32[64,1152]{1,0:T(8,128)}, f32[2,64,256]{2,1,0:T(8,128)}, f32[6,64,128]{2,1,0:T(8,128)}) custom-call(f32[9216,256]{1,0:T(8,128)} %g_hbm.1, f32[64,1152]{1,0:T(8,128)} %bitcast.3, f32[256,2048]{1,0:T(8,128)} %p_hbm.1), custom_call_target="tpu_custom_call" | custom-call | tf_op jit(solution)/shard_map/pallas_call | solution.py:667
  135.1 6.9 %shard_map.51 = (f32[64,256]{1,0:T(8,128)}, f32[64,1152]{1,0:T(8,128)}) custom-call(f32[64,1152]{1,0:T(8,128)} %get-tuple-element.7.n_ref, f32[2,64,256]{2,1,0:T(8,128)} %get-tuple-element.8.x_ref, f32[6,64,128]{2,1,0:T(8,128)} %get-tuple-element.9.m_ref), custom_call_target="tpu_custom_call" | custom-call | tf_op jit(solution)/shard_map/pallas_call | solution.py:698
